TPU v7x, 32 devices: a whole 2x2x4 slice. The times are simulated.
32 devices in a mesh: section: 2 (over y), dp: 16 (over z, x, core).
Axes of the slice: x: 2, y: 2, z: 4, core: 2. Of those that a mesh axis runs over, the one named last changes fastest.
Arguments:
- inputs: bfloat16 [2, 2048, 768], P(None, 'dp'), may hold values from -6 to 6
- cotangent: bfloat16 [2, 2048, 768], P(None, 'dp'), may hold values from -6 to 6
- markers: int32 [2, 2048], P(None, 'dp'), may hold values 0 or 1
- norm_gain: float32 [2, 768], P('section', 'dp'), may hold values from 0.5 to 1.5
- in_proj: float32 [2, 768, 3072], P('section', None, 'dp'), may hold values from -0.21875 to 0.21875
- conv_weight: float32 [2, 4, 1536], P('section', None, 'dp'), may hold values from -3 to 3
- conv_bias: float32 [2, 1536], P('section', 'dp'), may hold values from -3 to 3
- x_proj: float32 [2, 1536, 80], P('section', 'dp'), may hold values from -0.15625 to 0.15625
- dt_proj: float32 [2, 48, 1536], P('section', None, 'dp'), may hold values from -0.875 to 0.875
- dt_bias: float32 [2, 1536], P('section', 'dp'), may hold values from -6 to -2
- a_log: float32 [2, 1536, 16], P('section', 'dp'), may hold values from 0 to 2.77
- d_skip: float32 [2, 1536], P('section', 'dp'), may hold values from 0.5 to 1.5
- out_proj: float32 [2, 1536, 768], P('section', 'dp'), may hold values from -0.4375 to 0.4375
Outputs:
- section_out: bfloat16 [2, 2, 2048, 768], P('section', None, 'dp')
- section_grad: float32 [2, 2, 2048, 768], P('section', None, 'dp')
- grad_norm_gain: float32 [2, 768], P('section', 'dp')
- grad_in_proj: float32 [2, 768, 3072], P('section', None, 'dp')
- grad_conv_weight: float32 [2, 4, 1536], P('section', None, 'dp')
- grad_conv_bias: float32 [2, 1536], P('section', 'dp')
- grad_x_proj: float32 [2, 1536, 80], P('section', 'dp')
- grad_dt_proj: float32 [2, 48, 1536], P('section', None, 'dp')
- grad_dt_bias: float32 [2, 1536], P('section', 'dp')
- grad_a_log: float32 [2, 1536, 16], P('section', 'dp')
- grad_d_skip: float32 [2, 1536], P('section', 'dp')
- grad_out_proj: float32 [2, 1536, 768], P('section', 'dp')
All inputs are finite; a program needn't handle non-finite values. No bound on the sum of `markers` on one device may be relied on, other than what follows from the above.
Results may differ from a plain program's by a relative error of at most 0.017.
The roundings to bfloat16 on the way count: a program that leaves them out, or rounds other values in their place, can miss the bound.
Values may be sent and summed in bfloat16 or wider, within the bound.
A program may use at most 384 MiB of HBM per device.

v0:
```python
import jax
import jax.numpy as jnp
from jax import lax
from jax.sharding import PartitionSpec as P

KC = 4
BLK = 128


EPSILON = 1e-05


def shifted(value, axis, steps):
    count = lax.axis_size(axis)
    initial, last = (max(0, -steps), min(count, count - steps))
    return lax.ppermute(value, axis, [(source, source + steps) for source in range(initial, last)])


def combine(earlier, following):
    return (earlier[0] * following[0], following[0] * earlier[1] + following[1])


def delayed(values, delay_steps, fill_value):
    front_fill = jnp.full((delay_steps,) + values.shape[1:], fill_value, values.dtype)
    return jnp.concatenate([front_fill, values[: values.shape[0] - delay_steps]], axis=0)


def advanced(values, delay_steps):
    back_fill = jnp.zeros((delay_steps,) + values.shape[1:], values.dtype)
    return jnp.concatenate([values[delay_steps:], back_fill], axis=0)


def contract_rows(left_side, right_side):
    return lax.dot_general(
        left_side, right_side, (((0,), (0,)), ((), ())), preferred_element_type=jnp.float32
    )


def contract_cols(left_side, right_side):
    return lax.dot_general(
        left_side, right_side, (((1,), (1,)), ((), ())), preferred_element_type=jnp.float32
    )


def blocks_of(values):
    return values.reshape((values.shape[0] // BLK, BLK) + values.shape[1:])


def mask_list(resets_row):
    keep_masks = [jnp.ones_like(resets_row)]
    for offset in range(1, KC):
        keep_masks.append(keep_masks[-1] * (1.0 - delayed(resets_row, offset - 1, 1.0)))
    return keep_masks


def place_slot(buffer, values, slot_index, active):
    current = lax.dynamic_index_in_dim(buffer, slot_index, 0, keepdims=False)
    return lax.dynamic_update_index_in_dim(
        buffer, jnp.where(active, values, current), slot_index, 0
    )


def scan_forward(step_rate, act_f, resets_row, b_input, c_input, decay_rows):

    def block_step(carry_state, pieces):
        rate_blk, act_blk, reset_blk, b_blk, c_blk = pieces
        decay_factor = jnp.exp(rate_blk[:, None, :] * decay_rows) * (1.0 - reset_blk)[:, None, None]
        drive_term = (rate_blk * act_blk)[:, None, :] * b_blk[:, :, None]
        prefix_a, prefix_b = lax.associative_scan(combine, (decay_factor, drive_term), axis=0)
        states = prefix_a * carry_state + prefix_b
        return (states[-1], (carry_state, jnp.sum(states * c_blk[:, :, None], axis=1)))

    initial = jnp.zeros(decay_rows.shape, jnp.float32)
    pieces = tuple(
        (blocks_of(values) for values in (step_rate, act_f, resets_row, b_input, c_input))
    )
    final_state, (starts, scanned) = lax.scan(block_step, initial, pieces)
    return (starts, scanned.reshape(step_rate.shape))


def scan_backward(grad_ssm, step_rate, act_f, resets_row, b_input, c_input, decay_rows, starts):
    width = step_rate.shape[1]
    next_rate = jnp.concatenate([step_rate[1:], jnp.zeros((1, width), jnp.float32)], axis=0)
    next_reset = jnp.concatenate([resets_row[1:], jnp.ones((1,), jnp.float32)], axis=0)

    def block_step(carry_in, pieces):
        following, grad_a_neg = carry_in
        (
            grad_blk,
            rate_blk,
            act_blk,
            reset_blk,
            b_blk,
            c_blk,
            next_rate_blk,
            next_reset_blk,
            start_blk,
        ) = pieces
        decay_factor = jnp.exp(rate_blk[:, None, :] * decay_rows) * (1.0 - reset_blk)[:, None, None]
        drive_x = rate_blk * act_blk
        drive_term = drive_x[:, None, :] * b_blk[:, :, None]
        prefix_a, prefix_b = lax.associative_scan(combine, (decay_factor, drive_term), axis=0)
        states = prefix_a * start_blk + prefix_b
        before = jnp.concatenate([start_blk[None], states[:-1]], axis=0)
        multiplier = (
            jnp.exp(next_rate_blk[:, None, :] * decay_rows) * (1.0 - next_reset_blk)[:, None, None]
        )
        direct = grad_blk[:, None, :] * c_blk[:, :, None]
        suffix_a, suffix_b = lax.associative_scan(combine, (multiplier[::-1], direct[::-1]), axis=0)
        adjoint = (suffix_a * following + suffix_b)[::-1]
        exponent_grad = adjoint * before * decay_factor
        grad_rate = jnp.sum(exponent_grad * decay_rows, axis=1)
        grad_a_neg = grad_a_neg + jnp.sum(exponent_grad * rate_blk[:, None, :], axis=0)
        grad_drive = jnp.sum(adjoint * b_blk[:, :, None], axis=1)
        grad_b = jnp.sum(adjoint * drive_x[:, None, :], axis=2)
        grad_c = jnp.sum(grad_blk[:, None, :] * states, axis=2)
        return (
            (adjoint[0], grad_a_neg),
            (grad_rate + grad_drive * act_blk, grad_drive * rate_blk, grad_b, grad_c),
        )

    initial = (jnp.zeros(decay_rows.shape, jnp.float32), jnp.zeros(decay_rows.shape, jnp.float32))
    pieces = tuple(
        (
            blocks_of(values)
            for values in (
                grad_ssm,
                step_rate,
                act_f,
                resets_row,
                b_input,
                c_input,
                next_rate,
                next_reset,
            )
        )
    ) + (starts,)
    (following, grad_a_neg), block_outs = lax.scan(block_step, initial, pieces, reverse=True)
    flat = tuple((values.reshape((-1,) + values.shape[2:]) for values in block_outs))
    return flat + ((grad_a_neg * decay_rows).T,)


def forward_layer(resid_in, resets_row, weights):
    (
        norm_gain,
        in_proj,
        conv_weight,
        conv_bias,
        x_proj,
        dt_proj,
        dt_bias,
        a_log,
        d_skip,
        out_proj,
    ) = weights
    inner_width = conv_bias.shape[0]
    rank_width = dt_proj.shape[0]
    state_width = a_log.shape[1]
    inv_rms = lax.rsqrt(jnp.mean(resid_in * resid_in, axis=-1, keepdims=True) + EPSILON)
    normed = (resid_in * inv_rms * norm_gain).astype(jnp.bfloat16)
    mixed_out = jnp.dot(normed, in_proj, preferred_element_type=jnp.float32)
    x_part = mixed_out[:, :inner_width]
    z_part = mixed_out[:, inner_width:]
    keep_masks = mask_list(resets_row)
    conv_out = conv_bias + conv_weight[0] * x_part
    for offset in range(1, KC):
        conv_out = (
            conv_out
            + conv_weight[offset] * delayed(x_part, offset, 0.0) * keep_masks[offset][:, None]
        )
    activated = jax.nn.silu(conv_out).astype(jnp.bfloat16)
    act_f = activated.astype(jnp.float32)
    projected = jnp.dot(activated, x_proj, preferred_element_type=jnp.float32)
    rate_in = projected[:, :rank_width].astype(jnp.bfloat16)
    b_input = projected[:, rank_width : rank_width + state_width]
    c_input = projected[:, rank_width + state_width :]
    rate_pre = jnp.dot(rate_in, dt_proj, preferred_element_type=jnp.float32) + dt_bias
    step_rate = jax.nn.softplus(rate_pre)
    decay_rows = -jnp.exp(a_log).T
    starts, scanned = scan_forward(step_rate, act_f, resets_row, b_input, c_input, decay_rows)
    ssm_out = scanned + d_skip * act_f
    gated_out = (ssm_out * jax.nn.silu(z_part)).astype(jnp.bfloat16)
    result = resid_in + jnp.dot(gated_out, out_proj, preferred_element_type=jnp.float32)
    saved_state = (
        inv_rms,
        normed,
        mixed_out,
        conv_out,
        activated,
        rate_in,
        b_input,
        c_input,
        rate_pre,
        ssm_out,
        gated_out,
        starts,
    )
    return (result, saved_state)


def backward_inputs(grad_out, resid_in, resets_row, weights, saved_state):
    (
        norm_gain,
        in_proj,
        conv_weight,
        conv_bias,
        x_proj,
        dt_proj,
        dt_bias,
        a_log,
        d_skip,
        out_proj,
    ) = weights
    (
        inv_rms,
        normed,
        mixed_out,
        conv_out,
        activated,
        rate_in,
        b_input,
        c_input,
        rate_pre,
        ssm_out,
        gated_out,
        starts,
    ) = saved_state
    inner_width = conv_bias.shape[0]
    x_part = mixed_out[:, :inner_width]
    z_part = mixed_out[:, inner_width:]
    act_f = activated.astype(jnp.float32)
    step_rate = jax.nn.softplus(rate_pre)
    decay_rows = -jnp.exp(a_log).T
    out_low = grad_out.astype(jnp.bfloat16)
    grad_gated = contract_cols(out_low, out_proj)
    gate_sig = jax.nn.sigmoid(z_part)
    grad_ssm = grad_gated * z_part * gate_sig
    grad_z = grad_gated * ssm_out * gate_sig * (1.0 + z_part * (1.0 - gate_sig))
    grad_d_skip = jnp.sum(grad_ssm * act_f, axis=0)
    grad_rate, grad_act_scan, grad_b, grad_c, grad_a_log = scan_backward(
        grad_ssm, step_rate, act_f, resets_row, b_input, c_input, decay_rows, starts
    )
    grad_pre = (grad_rate * jax.nn.sigmoid(rate_pre)).astype(jnp.bfloat16)
    grad_dt_bias = jnp.sum(grad_pre.astype(jnp.float32), axis=0)
    grad_rate_in = contract_cols(grad_pre, dt_proj)
    grad_proj = jnp.concatenate([grad_rate_in, grad_b, grad_c], axis=1).astype(jnp.bfloat16)
    grad_act = grad_ssm * d_skip + grad_act_scan + contract_cols(grad_proj, x_proj)
    conv_sig = jax.nn.sigmoid(conv_out)
    grad_conv = grad_act * conv_sig * (1.0 + conv_out * (1.0 - conv_sig))
    grad_conv_bias = jnp.sum(grad_conv, axis=0)
    keep_masks = mask_list(resets_row)
    grad_x = grad_conv * conv_weight[0]
    weight_rows = [jnp.sum(grad_conv * x_part, axis=0)]
    for offset in range(1, KC):
        masked = grad_conv * keep_masks[offset][:, None]
        weight_rows.append(jnp.sum(masked * delayed(x_part, offset, 0.0), axis=0))
        grad_x = grad_x + advanced(masked, offset) * conv_weight[offset]
    grad_conv_weight = jnp.stack(weight_rows)
    grad_mixed = jnp.concatenate([grad_x, grad_z], axis=1).astype(jnp.bfloat16)
    grad_normed = contract_cols(grad_mixed, in_proj)
    grad_scaled = grad_normed * norm_gain
    grad_norm_gain = jnp.sum(grad_normed * resid_in * inv_rms, axis=0)
    cubed = inv_rms * inv_rms * inv_rms
    grad_in = (
        grad_out
        + inv_rms * grad_scaled
        - resid_in * cubed * jnp.mean(grad_scaled * resid_in, axis=-1, keepdims=True)
    )
    small_grads = (
        grad_norm_gain,
        grad_conv_weight,
        grad_conv_bias,
        grad_dt_bias,
        grad_a_log,
        grad_d_skip,
    )
    operands = (gated_out, out_low, rate_in, grad_pre, activated, grad_proj, normed, grad_mixed)
    return (grad_in, small_grads, operands)


def weight_products(small_grads, operands):
    gated_out, out_low, rate_in, grad_pre, activated, grad_proj, normed, grad_mixed = operands
    grad_out_proj = contract_rows(gated_out, out_low)
    grad_dt_proj = contract_rows(rate_in, grad_pre)
    grad_x_proj = contract_rows(activated, grad_proj)
    grad_in_proj = contract_rows(normed, grad_mixed)
    return (
        small_grads[0],
        grad_in_proj,
        small_grads[1],
        small_grads[2],
        grad_x_proj,
        grad_dt_proj,
        small_grads[3],
        small_grads[4],
        small_grads[5],
        grad_out_proj,
    )


def on_device(
    inputs,
    cotangent,
    markers,
    norm_gain,
    in_proj,
    conv_weight,
    conv_bias,
    x_proj,
    dt_proj,
    dt_bias,
    a_log,
    d_skip,
    out_proj,
):
    gathered = (
        lax.all_gather(norm_gain.astype(jnp.bfloat16), "dp", axis=1, tiled=True),
        lax.all_gather(in_proj.astype(jnp.bfloat16), "dp", axis=2, tiled=True),
        lax.all_gather(conv_weight.astype(jnp.bfloat16), "dp", axis=2, tiled=True),
        lax.all_gather(conv_bias.astype(jnp.bfloat16), "dp", axis=1, tiled=True),
        lax.all_gather(x_proj.astype(jnp.bfloat16), "dp", axis=1, tiled=True),
        lax.all_gather(dt_proj.astype(jnp.bfloat16), "dp", axis=2, tiled=True),
        lax.all_gather(dt_bias.astype(jnp.bfloat16), "dp", axis=1, tiled=True),
        lax.all_gather(a_log.astype(jnp.bfloat16), "dp", axis=1, tiled=True),
        lax.all_gather(d_skip.astype(jnp.bfloat16), "dp", axis=1, tiled=True),
        lax.all_gather(out_proj.astype(jnp.bfloat16), "dp", axis=1, tiled=True),
    )
    whole = tuple((gathered_piece[0] for gathered_piece in gathered))
    weights = (
        whole[0].astype(jnp.float32),
        whole[1],
        whole[2].astype(jnp.float32),
        whole[3].astype(jnp.float32),
        whole[4],
        whole[5],
        whole[6].astype(jnp.float32),
        whole[7].astype(jnp.float32),
        whole[8].astype(jnp.float32),
        whole[9],
    )
    section_index = lax.axis_index("section")
    last_section = lax.axis_size("section") - 1
    micro_count = inputs.shape[0]
    length = inputs.shape[1]
    first_pos = (jnp.arange(length) == 0)[None, :]
    resets = jnp.where((markers > 0) | first_pos, 1.0, 0.0).astype(jnp.float32)

    def run_forward(section_in, resets_row):
        return forward_layer(section_in, resets_row, weights)

    def skip_forward(section_in, resets_row):
        return jax.tree.map(jnp.zeros_like, forward_layer(section_in, resets_row, weights))

    received = jnp.zeros((length, inputs.shape[2]), jnp.bfloat16)
    section_out = jnp.zeros(inputs.shape, jnp.bfloat16)
    inputs_seen = jnp.zeros(inputs.shape, jnp.bfloat16)
    kept_store = None
    for tick_index in range(micro_count + 1):
        current = tick_index - section_index
        active = (current >= 0) & (current < micro_count)
        slot_index = jnp.clip(current, 0, micro_count - 1)
        entry_in = jnp.where(
            section_index == 0,
            lax.dynamic_index_in_dim(inputs, slot_index, 0, keepdims=False),
            received,
        )
        resets_row = lax.dynamic_index_in_dim(resets, slot_index, 0, keepdims=False)
        result, saved_state = lax.cond(
            active, run_forward, skip_forward, entry_in.astype(jnp.float32), resets_row
        )
        section_out = place_slot(section_out, result.astype(jnp.bfloat16), slot_index, active)
        inputs_seen = place_slot(inputs_seen, entry_in, slot_index, active)
        if kept_store is None:
            kept_store = jax.tree.map(
                lambda values: jnp.zeros((micro_count,) + values.shape, values.dtype), saved_state
            )
        kept_store = jax.tree.map(
            lambda buffer, values: place_slot(buffer, values, slot_index, active),
            kept_store,
            saved_state,
        )
        if tick_index < micro_count:
            received = shifted(result.astype(jnp.bfloat16), "section", 1)

    def run_inputs(grad_out, section_in, resets_row, slot_index):
        saved_state = jax.tree.map(
            lambda buffer: lax.dynamic_index_in_dim(buffer, slot_index, 0, keepdims=False),
            kept_store,
        )
        return backward_inputs(grad_out, section_in, resets_row, weights, saved_state)

    def run_full(grad_out, section_in, resets_row, slot_index):
        grad_in, small_grads, operands = run_inputs(grad_out, section_in, resets_row, slot_index)
        return (grad_in, weight_products(small_grads, operands))

    def skip_full(grad_out, section_in, resets_row, slot_index):
        return jax.tree.map(jnp.zeros_like, run_full(grad_out, section_in, resets_row, slot_index))

    grad_back = jnp.zeros((length, inputs.shape[2]), jnp.bfloat16)
    section_grad = jnp.zeros(inputs.shape, jnp.float32)
    totals = None
    for tick_index in range(micro_count + 1):
        current = tick_index - (last_section - section_index)
        active = (current >= 0) & (current < micro_count)
        slot_index = jnp.clip(current, 0, micro_count - 1)
        grad_out = jnp.where(
            section_index == last_section,
            lax.dynamic_index_in_dim(cotangent, slot_index, 0, keepdims=False),
            grad_back,
        ).astype(jnp.float32)
        section_in = lax.dynamic_index_in_dim(inputs_seen, slot_index, 0, keepdims=False).astype(
            jnp.float32
        )
        resets_row = lax.dynamic_index_in_dim(resets, slot_index, 0, keepdims=False)
        grad_in, weight_grads = lax.cond(
            active, run_full, skip_full, grad_out, section_in, resets_row, slot_index
        )
        section_grad = place_slot(section_grad, grad_in, slot_index, active)
        if tick_index < micro_count:
            grad_back = shifted(grad_in.astype(jnp.bfloat16), "section", -1)
        totals = (
            weight_grads
            if totals is None
            else tuple((older + newer for older, newer in zip(totals, weight_grads)))
        )
    totals = (
        lax.psum_scatter(totals[0][None], "dp", scatter_dimension=1, tiled=True),
        lax.psum_scatter(totals[1][None], "dp", scatter_dimension=2, tiled=True),
        lax.psum_scatter(totals[2][None], "dp", scatter_dimension=2, tiled=True),
        lax.psum_scatter(totals[3][None], "dp", scatter_dimension=1, tiled=True),
        lax.psum_scatter(totals[4][None], "dp", scatter_dimension=1, tiled=True),
        lax.psum_scatter(totals[5][None], "dp", scatter_dimension=2, tiled=True),
        lax.psum_scatter(totals[6][None], "dp", scatter_dimension=1, tiled=True),
        lax.psum_scatter(totals[7][None], "dp", scatter_dimension=1, tiled=True),
        lax.psum_scatter(totals[8][None], "dp", scatter_dimension=1, tiled=True),
        lax.psum_scatter(totals[9][None], "dp", scatter_dimension=1, tiled=True),
    )
    return (
        section_out[None],
        section_grad[None],
        totals[0],
        totals[1],
        totals[2],
        totals[3],
        totals[4],
        totals[5],
        totals[6],
        totals[7],
        totals[8],
        totals[9],
    )


def solution(mesh):
    placed = (
        P(None, "dp", None),
        P(None, "dp", None),
        P(None, "dp"),
        P("section", "dp"),
        P("section", None, "dp"),
        P("section", None, "dp"),
        P("section", "dp"),
        P("section", "dp", None),
        P("section", None, "dp"),
        P("section", "dp"),
        P("section", "dp", None),
        P("section", "dp"),
        P("section", "dp", None),
    )
    return jax.shard_map(
        on_device,
        mesh=mesh,
        in_specs=placed,
        out_specs=(
            P("section", None, "dp", None),
            P("section", None, "dp", None),
            P("section", "dp"),
            P("section", None, "dp"),
            P("section", None, "dp"),
            P("section", "dp"),
            P("section", "dp", None),
            P("section", None, "dp"),
            P("section", "dp"),
            P("section", "dp", None),
            P("section", "dp"),
            P("section", "dp", None),
        ),
        check_vma=False,
    )
```

profile of v0, /device:TPU:0, one launch (start us, length us, event | category | flops | bytes accessed | tf_op | source)
XLA Modules:
  0.0 5307.7 jit_solution(11436568179485281440)
XLA Ops:
  18.2 63.4 %all-reduce.292 = (bf16[768]{0:T(1024)(128)(2,1)S(1)}, bf16[1536]{0:T(1024)(128)(2,1)S(1)}, bf16[1536]{0:T(1024)(128)(2,1)S(1)}, bf16[1536]{0:T(1024)(128)(2,1)S(1)}) all-reduce(bf16[768]{0:T(1024)(128)(2,1)S(1)} %dynamic-update-slice, bf16[1536]{0:T(1024)(128)(2,1)S(1)} %dynamic-update-slice.1, ...), channel_id=1, replica_groups=mesh['section'=2,'dp'=16] {'dp'}, use_global_device_ids=true, to_apply=%add.288 | all-reduce | flops 5376 | bytes 21504
  84.8 22.8 all_gather.33
  108.4 22.5 all_gather.37
  152.9 21.1 all_gather.34
  178.4 457.5 %conditional.6 = (f32[128,1]{0,1:T(1,128)}, bf16[128,768]{1,0:T(8,128)(2,1)}, f32[128,3072]{1,0:T(8,128)S(1)}, f32[128,1536]{1,0:T(8,128)}, bf16[128,1536]{1,0:T...) conditional(s32[]{:T(128)} %convert_element_type.371, ...), branch_computations={%region_0.1_spmd, %region_1.4_spmd} | conditional | flops 1028604928 | bytes 871680640 | solution.py:368
  374.4 20.1 pad.1397
  394.5 20.2 pad.1411
  456.8 38.5 pad.1412
  495.3 38.5 pad.1398
  533.8 38.6 pad.1399
  572.4 38.6 pad.1413
  611.0 20.4 multiply_reduce_fusion
  665.1 457.5 %conditional.7 = (f32[128,1]{0,1:T(1,128)}, bf16[128,768]{1,0:T(8,128)(2,1)}, f32[128,3072]{1,0:T(8,128)S(1)}, f32[128,1536]{1,0:T(8,128)}, bf16[128,1536]{1,0:T...) conditional(s32[]{:T(128)} %convert_element_type.396, ...), branch_computations={%region_4.5_spmd, %region_5.8_spmd} | conditional | flops 1028310016 | bytes 873056896 | solution.py:368
  861.6 20.1 pad.1425
  881.6 20.2 pad.1439
  943.9 38.5 pad.1440
  982.5 38.5 pad.1426
  1021.0 38.6 pad.1427
  1059.6 38.6 pad.1441
  1098.2 20.9 multiply_reduce_fusion.1
  1193.5 1427.3 %collective-permute-done.2 = bf16[128,768]{1,0:T(8,128)(2,1)S(1)} collective-permute-done((bf16[128,768]{1,0:T(8,128)(2,1)S(1)}, bf16[128,768]{1,0:T(8,128)(2,1)S(1)}, u32[]{:S(2)}, u32[]{:S(2)}) %collective-permute-start.2) | collective-permute-done | bytes 196640 | tf_op jit(solution)/shard_map/ppermute | solution.py:16
  2621.7 1002.7 %conditional.10 = (f32[128,768]{1,0:T(8,128)S(1)}, f32[768]{0:T(1024)S(1)}, f32[4,1536]{1,0:T(4,128)S(1)}, f32[1536]{0:T(1024)S(1)}, f32[1536,80]{0,1:T(8,128)S(...) conditional(s32[]{:T(128)} %convert_element_type.403, ...), branch_computations={%region_28.29_spmd, %region_29.44_spmd} | conditional | flops 2096662656 | bytes 1896291968 | solution.py:415
  2828.7 20.2 pad.1578
  2862.0 20.1 pad.1565
  2882.1 20.2 pad.1579
  2943.9 38.5 pad.1580
  2982.5 38.5 pad.1566
  3021.0 38.6 pad.1567
  3059.6 38.6 pad.1581
  3098.2 26.3 multiply_reduce_fusion.6
  3287.7 20.2 pad.1550
  3321.0 20.0 pad.1537
  3341.0 20.2 pad.1551
  3401.6 38.5 pad.1552
  3440.1 38.5 pad.1538
  3478.7 38.6 pad.1539
  3517.3 38.6 pad.1553
  3555.8 23.7 add_add_fusion.1
  3634.4 1003.5 %conditional.11 = (f32[128,768]{1,0:T(8,128)}, f32[768]{0:T(1024)S(1)}, f32[4,1536]{1,0:T(4,128)}, f32[1536]{0:T(1024)}, f32[1536,80]{0,1:T(8,128)}, /*index=5*/...) conditional(s32[]{:T(128)} %convert_element_type.406, ...), branch_computations={%region_44.45_spmd, %region_45.60_spmd} | conditional | flops 2096662656 | bytes 1914207872 | solution.py:415
  3842.0 20.2 pad.1634
  3875.4 20.1 pad.1621
  3895.5 20.2 pad.1635
  3956.3 38.5 pad.1636
  3994.8 38.5 pad.1622
  4033.4 38.6 pad.1623
  4071.9 38.6 pad.1637
  4110.5 26.3 multiply_reduce_fusion.14
  4300.4 20.2 pad.1606
  4333.7 20.0 pad.1593
  4353.7 20.2 pad.1607
  4414.4 38.5 pad.1608
  4452.9 38.5 pad.1594
  4491.4 38.6 pad.1595
  4530.0 38.6 pad.1609
  4568.6 23.7 add_add_fusion.3
  4692.5 58.1 %reduce-scatter.35.cloned.1.call-done = f32[96,1]{1,0:T(8,128)} async-done(((f32[1536,1]{1,0:T(8,128)}), f32[96,1]{1,0:T(8,128)}) %reduce-scatter.35.cloned.1.call-update) | async-done | bytes 400
  4751.9 57.6 %reduce-scatter.41.cloned.1.call-done = f32[96,1]{1,0:T(8,128)} async-done(((f32[1536,1]{1,0:T(8,128)}), f32[96,1]{1,0:T(8,128)}) %reduce-scatter.41.cloned.1.call-update) | async-done | bytes 400
  4810.9 58.0 %reduce-scatter.45.cloned.1.call-done = f32[96,1]{1,0:T(8,128)} async-done(((f32[1536,1]{1,0:T(8,128)}), f32[96,1]{1,0:T(8,128)}) %reduce-scatter.45.cloned.1.call-update) | async-done | bytes 400
  4870.3 57.7 %reduce-scatter.33.cloned.1.call-done = f32[96,4]{1,0:T(8,128)} async-done(((f32[1536,4]{1,0:T(8,128)}), f32[96,4]{1,0:T(8,128)}) %reduce-scatter.33.cloned.1.call-update) | async-done | bytes 1552
  4929.5 58.1 %reduce-scatter.43.cloned.1.call-done = f32[96,16]{1,0:T(8,128)} async-done(((f32[1536,16]{1,0:T(8,128)}), f32[96,16]{1,0:T(8,128)}) %reduce-scatter.43.cloned.1.call-update) | async-done | bytes 6160
  4989.0 57.6 %reduce-scatter.39.cloned.1.call-done = f32[96,48]{1,0:T(8,128)} async-done(((f32[1536,48]{1,0:T(8,128)}), f32[96,48]{1,0:T(8,128)}) %reduce-scatter.39.cloned.1.call-update) | async-done | bytes 18448
  5048.1 57.9 %reduce-scatter.37.cloned.1.call-done = f32[96,80]{1,0:T(8,128)} async-done(((f32[1536,80]{1,0:T(8,128)}), f32[96,80]{1,0:T(8,128)}) %reduce-scatter.37.cloned.1.call-update) | async-done | bytes 30736
  5107.5 77.5 %reduce-scatter.29.cloned.1.call-done = f32[1,96,768]{2,1,0:T(8,128)} async-done(((f32[1,1536,768]{2,1,0:T(8,128)}), f32[1,96,768]{2,1,0:T(8,128)}) %reduce-scatter.29.cloned.1.call-update) | async-done | bytes 294928 | tf_op jit(solution)/shard_map/reduce_scatter | solution.py:436
  5185.0 115.6 %reduce-scatter.27.cloned.1.call-done = f32[1,768,192]{1,2,0:T(8,128)} async-done(((f32[1,768,3072]{1,2,0:T(8,128)}), f32[1,768,192]{1,2,0:T(8,128)}) %reduce-scatter.27.cloned.1.call-update) | async-done | bytes 589840 | tf_op jit(solution)/shard_map/reduce_scatter | solution.py:428
  (1621 shorter events, 1756.8 us)
Async XLA Ops:
  7.2 171.2 %all-gather.5.cloned.1.call-start = ((), (), s32[]{:S(2)}) async-start(), calls=%async_computation.11 | async-start | bytes 2506752 | tf_op jit(solution)/shard_map/all_gather | solution.py:326
  8.9 169.5 %all-gather.3.cloned.1.call-start = ((), (), s32[]{:S(2)}) async-start(), calls=%async_computation.10 | async-start | bytes 5013504 | tf_op jit(solution)/shard_map/all_gather | solution.py:318
  10.8 4680.4 %reduce-scatter.31.cloned.1.call-start = ((), (), s32[]{:S(2)}) async-start(), calls=%async_computation.14 | async-start | bytes 417792
  81.6 1072.2 %copy-start.449 = (f32[768]{0:T(1024)}, f32[768]{0:T(1024)S(1)}, u32[]{:S(2)}) copy-start(f32[768]{0:T(1024)S(1)} %convert_element_type.434) | copy-start | bytes 9220
  82.2 582.9 %copy-start.469 = (f32[1536]{0:T(1024)}, f32[1536]{0:T(1024)S(1)}, u32[]{:S(2)}) copy-start(f32[1536]{0:T(1024)S(1)} %convert_element_type.435) | copy-start | bytes 18436
  108.4 70.0 %copy-start.33 = (f32[1,4,1536]{1,0,2:T(1,128)}, f32[1,4,1536]{1,0,2:T(1,128)S(1)}, u32[]{:S(2)}) copy-start(f32[1,4,1536]{1,0,2:T(1,128)S(1)} %convert_element_type.430) | copy-start | bytes 73732
  108.4 67.2 %copy-start.301 = (bf16[2,128,768]{2,1,0:T(8,128)(2,1)S(1)}, bf16[2,128,768]{2,1,0:T(8,128)(2,1)}, u32[]{:S(2)}) copy-start(bf16[2,128,768]{2,1,0:T(8,128)(2,1)} %param.25) | copy-start | bytes 1179652
  130.9 46.9 copy-start.528
  131.7 46.6 copy-start.37
  188.9 442.5 %copy-start.162 = (bf16[128,1536]{1,0:T(8,128)(2,1)}, bf16[128,1536]{1,0:T(8,128)(2,1)S(1)}, u32[]{:S(2)}) copy-start(bf16[128,1536]{1,0:T(8,128)(2,1)S(1)} %get-tuple-element.2663) | copy-start | bytes 1179652 | tf_op jit(solution)/shard_map/cond
  394.5 48.8 slice-start.9
  414.6 28.7 slice-start.10
  434.0 19.7 slice-start.39
  572.4 38.6 copy-start.440
  611.0 20.4 copy-start.42
  611.0 20.4 copy-start.463
  640.3 24.0 collective-permute-start
  675.8 443.3 %copy-start.164 = (bf16[128,1536]{1,0:T(8,128)(2,1)}, bf16[128,1536]{1,0:T(8,128)(2,1)S(1)}, u32[]{:S(2)}) copy-start(bf16[128,1536]{1,0:T(8,128)(2,1)S(1)} %get-tuple-element.2689) | copy-start | bytes 1179652 | tf_op jit(solution)/shard_map/cond
  881.6 48.8 slice-start.11
  901.8 28.7 slice-start.12
  921.1 19.7 slice-start.41
  1059.6 38.6 copy-start.441
  1098.2 20.9 copy-start.45
  1098.2 20.9 copy-start.464
  1098.2 22.2 copy-start.78
  1122.6 18.1 copy-start.105
  1122.6 18.1 copy-start.286
  1133.2 19.7 collective-permute-start.1
  1192.2 1428.6 %collective-permute-start.2 = (bf16[128,768]{1,0:T(8,128)(2,1)S(1)}, bf16[128,768]{1,0:T(8,128)(2,1)S(1)}, u32[]{:S(2)}, u32[]{:S(2)}) collective-permute-start(bf16[128,768]{1,0:T(8,128)(2,1)S(1)} %convert_element_type.404), channel_id=1, source_target_pairs={{16,0},{17,1},{18,2},{19,3},{20,4},{21,5},{22,6},{23,7},{24,8},{25... | collective-permute-start | bytes 589832 | tf_op jit(solution)/shard_map/ppermute | solution.py:16
  2621.7 25.1 copy-start.271
  2621.7 17.3 copy-start.81
  2621.7 17.3 copy-start.100
  2882.1 48.4 slice-start.19
  2902.2 28.3 slice-start.20
  2921.1 19.8 slice-start.49
  3059.6 38.6 copy-start.331
  3059.6 38.6 copy-start.438
  3059.6 38.6 copy-start.447
  3126.7 18.0 slice-start.35
  3341.0 48.4 slice-start.21
  3361.1 28.2 slice-start.22
  3625.5 7.9 collective-permute-start.3
  3634.8 25.0 copy-start.269
  3634.8 17.2 copy-start.82
  3634.8 17.2 copy-start.102
  3895.4 48.5 slice-start.23
  3915.6 28.3 slice-start.24
  4071.9 38.6 copy-start.332
  4071.9 38.6 copy-start.439
  4071.9 38.6 copy-start.448
  4139.0 18.0 slice-start.37
  4353.7 48.5 slice-start.25
  4373.9 28.3 slice-start.26
  4639.5 111.0 %reduce-scatter.35.cloned.1.call-start = ((), (), s32[]{:S(2)}) async-start(), calls=%async_computation.16 | async-start | bytes 835584
  4641.6 168.0 %reduce-scatter.41.cloned.1.call-start = ((), (), s32[]{:S(2)}) async-start(), calls=%async_computation.19 | async-start | bytes 835584
  4643.5 225.4 %reduce-scatter.45.cloned.1.call-start = ((), (), s32[]{:S(2)}) async-start(), calls=%async_computation.21 | async-start | bytes 835584
  4645.6 282.5 %reduce-scatter.33.cloned.1.call-start = ((), (), s32[]{:S(2)}) async-start(), calls=%async_computation.15 | async-start | bytes 835584
  4648.2 339.4 %reduce-scatter.43.cloned.1.call-start = ((), (), s32[]{:S(2)}) async-start(), calls=%async_computation.20 | async-start | bytes 835584
  4651.0 395.7 %reduce-scatter.39.cloned.1.call-start = ((), (), s32[]{:S(2)}) async-start(), calls=%async_computation.18 | async-start | bytes 835584
  4653.8 452.1 %reduce-scatter.37.cloned.1.call-start = ((), (), s32[]{:S(2)}) async-start(), calls=%async_computation.17 | async-start | bytes 835584
  4656.8 528.2 %reduce-scatter.29.cloned.1.call-start = ((), (), s32[]{:S(2)}) async-start(), calls=%async_computation.13 | async-start | bytes 5013504 | tf_op jit(solution)/shard_map/reduce_scatter | solution.py:436
  4665.0 635.6 %reduce-scatter.27.cloned.1.call-start = ((), (), s32[]{:S(2)}) async-start(), calls=%async_computation.12 | async-start | bytes 10027008 | tf_op jit(solution)/shard_map/reduce_scatter | solution.py:428
  4681.4 619.2 %copy-start.373 = (bf16[1,2,128,768]{3,2,1,0:T(8,128)(2,1)}, bf16[1,2,128,768]{3,2,1,0:T(8,128)(2,1)S(1)}, u32[]{:S(2)}) copy-start(bf16[1,2,128,768]{3,2,1,0:T(8,128)(2,1)S(1)} %bitcast_dynamic-update-slice_fusion.26) | copy-start | bytes 1179652
  4682.6 618.0 %copy-start.333 = (f32[1,2,128,768]{3,2,1,0:T(8,128)}, f32[1,2,128,768]{3,2,1,0:T(8,128)S(1)}, u32[]{:S(2)}) copy-start(f32[1,2,128,768]{3,2,1,0:T(8,128)S(1)} %bitcast_dynamic-update-slice_fusion.12) | copy-start | bytes 2359300
  (385 other events, 1666.8 us)
Sparse Core Ops, SparseCore 0:
  10.9 45.2 all-gather.4
  59.0 57.1 all-gather.2
  4639.6 51.4 reduce-scatter.30
  4695.0 55.5 reduce-scatter.34
  4753.9 55.5 reduce-scatter.40
  4813.4 55.5 reduce-scatter.44
  4872.5 55.5 reduce-scatter.32
  4932.0 55.5 reduce-scatter.42
  4991.1 55.4 reduce-scatter.38
  5050.4 55.4 reduce-scatter.36
  5110.4 74.5 reduce-scatter.28
  5190.1 110.4 reduce-scatter.26
where the time goes:
time: 5380 us; the launch traced here: 5310 us
  local copies, waits for them, and re-layouts  2170 us (40%)
  waiting for transfers between devices  2040 us (38%)
  other arithmetic  858 us (16%)
  blocking collectives  149 us (3%)
  matrix products  57.3 us (1%)
    ppermute x4, waiting for transfers between devices, shifted(): lax.ppermute(value, axis, [(source, source + steps) for source in range(i...  1430 us
    pad x96, local copies, waits for them, and re-layouts, block_step(): lax.associative_scan(combine, (decay_factor, drive_term), axis=0)  1230 us
    pad x48, local copies, waits for them, and re-layouts, block_step(): lax.associative_scan(combine, (multiplier[::-1], direct[::-1]), axis=0)  623 us
    unnamed x20, waiting for transfers between devices  414 us
    mul x72, other arithmetic, combine(): return (earlier[0] * following[0], following[0] * earlier[1] + following[1])  284 us
    reduce_scatter x1, waiting for transfers between devices, on_device(): lax.psum_scatter(totals[1][None], 'dp', scatter_dimension=2, tiled=True)  116 us
  transfers between devices with their start and end apart: 16, of which 12 were waited for; matrix products, arithmetic and copies ran while one was open for 2% of the time, Pallas kernels for 0%

commit v1 on v0

v1 whole, which is shorter than its diff:
```python
import functools
import types

import jax
import jax.numpy as jnp
from jax import lax
from jax.experimental import pallas as pl
from jax.experimental.pallas import tpu as pltpu
from jax.sharding import PartitionSpec as P

T = 128
D = 768
DI = 1536
NS = 16
KC = 4
RK = 48
MICRO = 2
C = 512
CS = 768
TB = 16
NB = T // TB
EPS = 1e-5
LOG2E = 1.4426950408889634
LN2 = 0.6931471805599453
BIG = 1e30
GAIN_LANE = 24
DP, SECTION = "dp", "section"
UP, DOWN, ACROSS, CORE = range(4)
BELOW, ABOVE = range(2)
START, FORWARD, FINISH = range(3)
RIGHT, LEFT = range(2)
f32 = jnp.float32
bf16 = jnp.bfloat16


def nn(a, b):
    return lax.dot_general(a, b, (((1,), (0,)), ((), ())), preferred_element_type=f32)


def nt(a, b):
    return lax.dot_general(a, b, (((1,), (1,)), ((), ())), preferred_element_type=f32)


def tn(a, b):
    return lax.dot_general(a, b, (((0,), (0,)), ((), ())), preferred_element_type=f32)


def iota(shape, axis):
    return lax.broadcasted_iota(jnp.int32, shape, axis)


def sigmoid(v):
    return 1.0 / (1.0 + jnp.exp(-v))


def softplus(v):
    return jnp.maximum(v, 0.0) + jnp.log1p(jnp.exp(-jnp.abs(v)))


def wide(v):
    return jnp.concatenate([v] * (CS // 128), axis=1)


def keeps(reset):
    keep = [None]
    cur = jnp.ones_like(reset)
    for k in range(1, KC):
        cur = cur * (1.0 - (reset if k == 1 else pltpu.roll(reset, k - 1, 0)))
        keep.append(cur)
    return keep


def block_diagonal(cols):
    tile = (iota((NS, NS * TB), 1) % NS == iota((NS, NS * TB), 0)).astype(bf16)
    rep = nn(cols.astype(bf16), tile)
    own = (iota((T, NS * TB), 1) // NS) == (iota((T, NS * TB), 0) % TB)
    return jnp.where(own, rep, 0.0).astype(bf16)


def lane_columns(dst, val):
    for t in range(T):
        dst[pl.ds(t * NS, NS), :] = jnp.broadcast_to(val[:, t : t + 1], (NS, 128))


def f_x(reset, normed, win, rows, x_ref, act):
    keep = keeps(reset)
    for c in range(DI // C):
        s = pl.ds(c * C, C)
        x = nt(normed[...], win[s, :])
        x_ref[:, s] = x
        v = rows[20:21, s] + rows[16:17, s] * x
        for k in range(1, KC):
            v = v + rows[16 + k : 17 + k, s] * (pltpu.roll(x, k, 0) * keep[k])
        act[:, s] = (v * sigmoid(v)).astype(bf16)


def f_rate(reset, act, small, rows, proj, rin, pre_ref, dec, drive, cols, diag):
    p = nn(act[...], small[:, 0:128])
    proj[...] = p
    lane_columns(cols, p.T[RK : RK + NS, :])
    diag[...] = block_diagonal(p[:, RK + NS : RK + 2 * NS])
    rin[...] = pltpu.roll(jnp.where(iota((T, 128), 1) < RK, p, 0.0), RK + 2 * NS, 1).astype(bf16)
    for c in range(DI // C):
        s = pl.ds(c * C, C)
        pre = nt(rin[...], small[s, 0:128]) + rows[21:22, s]
        pre_ref[:, s] = pre
        rate = softplus(pre)
        dec[:, s] = jnp.where(reset > 0.0, BIG, rate)
        drive[:, s] = rate * act[:, s].astype(f32)


def f_scan(act, rows, dec, drive, cols, diag, h_ref, ssm):
    h_ref[0:NS, :] = jnp.zeros((NS, DI), bf16)
    for c in range(DI // CS):
        s = pl.ds(c * CS, CS)

        def block(i, h):
            t0 = pl.multiple_of(i * TB, TB)
            a2 = rows[0:NS, s]
            d = dec[pl.ds(t0, TB), s]
            v = drive[pl.ds(t0, TB), s]
            for j in range(TB):
                b = wide(cols[pl.ds(t0 * NS + j * NS, NS), :])
                h = jnp.exp2(d[j : j + 1, :] * a2) * h + v[j : j + 1, :] * b
                h_ref[pl.ds(t0 * NS + (j + 1) * NS, NS), s] = h.astype(bf16)
            return h

        lax.fori_loop(0, NB, block, jnp.zeros((NS, CS), f32))

    def sums(i, carry):
        for q in range(4):
            t0 = pl.multiple_of(i * (4 * TB) + q * TB, TB)
            tt = pl.ds(t0, TB)
            y = nn(diag[tt, :], h_ref[pl.ds(t0 * NS + NS, TB * NS), :])
            ssm[tt, :] = y + rows[22:23, :] * act[tt, :].astype(f32)
        return carry

    lax.fori_loop(0, NB // 4, sums, 0)


def f_out(u, normed, win, wout, ssm, z_ref, gated, out):
    acc = u[...].astype(f32)
    for c in range(DI // C):
        s = pl.ds(c * C, C)
        z = nt(normed[...], win[pl.ds(DI + c * C, C), :])
        z_ref[:, s] = z
        g = (ssm[:, s] * (z * sigmoid(z))).astype(bf16)
        gated[:, s] = g
        acc = acc + nn(g, wout[s, :])
    out[...] = acc.astype(bf16)


def total(old, first, value):
    return jnp.where(first, value, old + value)


def b_gate(first, go_ref, wout, z_ref, ssm, act, gs_ref, gm, sm):
    go = go_ref[...]
    for c in range(DI // C):
        s = pl.ds(c * C, C)
        gg = nt(go, wout[s, :])
        z = z_ref[:, s]
        sg = sigmoid(z)
        gs = gg * z * sg
        gs_ref[:, s] = gs
        gm[:, pl.ds(DI + c * C, C)] = (gg * ssm[:, s] * sg * (1.0 + z * (1.0 - sg))).astype(bf16)
        part = jnp.sum(gs * act[:, s].astype(f32), axis=0, keepdims=True)
        sm[22:23, s] = total(sm[22:23, s], first, part)


def b_prep(reset, pre, act, proj, dec, drive, cols, diag):
    p = proj[...]
    lane_columns(cols, p.T[RK + NS : RK + 2 * NS, :])
    diag[...] = block_diagonal(p[:, RK : RK + NS])
    for c in range(DI // C):
        s = pl.ds(c * C, C)
        rate = softplus(pre[:, s])
        dec[:, s] = jnp.where(reset > 0.0, BIG, rate)
        drive[:, s] = (rate * act[:, s].astype(f32)).astype(bf16)


def b_scan(first, gs, rows, dec, cols, diag, drive, h_ref, adj_ref, gd, gr, gb, gc, sm):
    ones = (iota((TB, TB * NS), 1) // NS) == iota((TB, TB * NS), 0)
    od = ones.astype(bf16)

    def state_sums(i, carry):
        for q in range(4):
            t0 = pl.multiple_of(i * (4 * TB) + q * TB, TB)
            tt = pl.ds(t0, TB)
            full = nt(gs[tt, :].astype(bf16), h_ref[pl.ds(t0 * NS + NS, TB * NS), :])
            gc[tt, :] = jnp.where(ones, full, 0.0).astype(bf16)
        return carry

    lax.fori_loop(0, NB // 4, state_sums, 0)
    for c in range(DI // CS):
        s = pl.ds(c * CS, CS)

        def block(i, state):
            carry, acc = state
            t0 = pl.multiple_of((NB - 1 - i) * TB, TB)
            a2 = rows[0:NS, s]
            d = dec[pl.ds(t0, TB), s]
            g = gs[pl.ds(t0, TB), s]
            for j in reversed(range(TB)):
                row = pl.ds(t0 * NS + j * NS, NS)
                adj = g[j : j + 1, :] * wide(cols[row, :]) + carry
                adj_ref[row, :] = adj.astype(bf16)
                dj = d[j : j + 1, :]
                carry = jnp.exp2(dj * a2) * adj
                expo = carry * h_ref[row, s].astype(f32)
                h_ref[row, s] = (expo * a2).astype(bf16)
                acc = acc + expo * dj
            return carry, acc

        zero = jnp.zeros((NS, CS), f32)
        _, acc = lax.fori_loop(0, NB, block, (zero, zero))
        sm[0:NS, s] = total(sm[0:NS, s], first, acc * rows[0:NS, s] * LN2)

        def adjoint_sums(i, carry):
            for q in range(4):
                t0 = pl.multiple_of(i * (4 * TB) + q * TB, TB)
                tt = pl.ds(t0, TB)
                row = pl.ds(t0 * NS, TB * NS)
                gd[tt, s] = nn(diag[tt, :], adj_ref[row, :])
                gr[tt, s] = nn(od, h_ref[row, s]) * LN2
                full = nt(drive[tt, s], adj_ref[row, :])
                gb[tt, :] = full if c == 0 else gb[tt, :] + full
            return carry

        lax.fori_loop(0, NB // 4, adjoint_sums, 0)


def b_pre(first, act, pre, small, gd, gr, gb, gc, gpre, gp, sm):
    acc = jnp.zeros((T, 128), f32)
    for c in range(DI // C):
        s = pl.ds(c * C, C)
        g = ((gr[:, s] + gd[:, s] * act[:, s].astype(f32)) * sigmoid(pre[:, s])).astype(bf16)
        gpre[:, s] = g
        part = jnp.sum(g.astype(f32), axis=0, keepdims=True)
        sm[21:22, s] = total(sm[21:22, s], first, part)
        acc = acc + nn(g, small[s, 0:128])
    k = iota((TB * NS, 128), 0) % NS
    lane = iota((TB * NS, 128), 1)
    own = (iota((T, NS * TB), 1) // NS) == (iota((T, NS * TB), 0) % TB)
    gb_own = jnp.where(own, gb[...], 0.0).astype(bf16)
    bc = nn(gb_own, (lane == RK + k).astype(bf16)) + nn(gc[...], (lane == RK + NS + k).astype(bf16))
    gp[...] = jnp.where(iota((T, 128), 1) < RK, pltpu.roll(acc, RK, 1), bc).astype(bf16)


def b_conv(first, reset, rows, small, x_ref, gs, gd, pre, gp, gm, sm):
    keep = keeps(reset)
    for c in range(DI // C):
        s = pl.ds(c * C, C)
        x = x_ref[:, s]
        xs = [x] + [pltpu.roll(x, k, 0) * keep[k] for k in range(1, KC)]
        v = rows[20:21, s]
        for k in range(KC):
            v = v + rows[16 + k : 17 + k, s] * xs[k]
        ga = gs[:, s] * rows[22:23, s] + gd[:, s] * softplus(pre[:, s]) + nt(gp[...], small[s, 0:128])
        sg = sigmoid(v)
        gc = ga * sg * (1.0 + v * (1.0 - sg))
        part = jnp.sum(gc, axis=0, keepdims=True)
        sm[20:21, s] = total(sm[20:21, s], first, part)
        gx = gc * rows[16:17, s]
        for k in range(KC):
            part = jnp.sum(gc * xs[k], axis=0, keepdims=True)
            sm[16 + k : 17 + k, s] = total(sm[16 + k : 17 + k, s], first, part)
            if k:
                gx = gx + pltpu.roll(gc * keep[k], T - k, 0) * rows[16 + k : 17 + k, s]
        gm[:, s] = gx.astype(bf16)


def b_in(first, u_ref, go_ref, gain, win, gm, sg, gg):
    gn = jnp.zeros((T, D), f32)
    for c in range(2 * DI // C):
        s = pl.ds(c * C, C)
        gn = gn + nn(gm[:, s], win[s, :])
    u = u_ref[...].astype(f32)
    inv = lax.rsqrt(jnp.mean(u * u, axis=-1, keepdims=True) + EPS)
    g = gn * gain[...]
    gg[...] = total(gg[...], first, jnp.sum(gn * u * inv, axis=0, keepdims=True))
    mean = jnp.mean(g * u, axis=-1, keepdims=True)
    sg[...] = go_ref[...].astype(f32) + inv * g - u * (inv * inv * inv) * mean


class Links:
    def __init__(self, n):
        self.zs = n // 4
        i = lax.axis_index(DP)
        self.i = i
        self.c = i % 2
        self.x = (i // 2) % 2
        self.z = i // 4

    def owner(self, z, x, c):
        return 4 * z + 2 * x + c

    def dev(self, route):
        step = (4, -4, 2 - 4 * self.x, 1 - 2 * self.c)[route]
        return dict(dp=self.i + step)

    def barrier(self):
        sem = pltpu.get_barrier_semaphore()

        def tell(device):
            pl.semaphore_signal(sem, inc=1, device_id=device, device_id_type=pl.DeviceIdType.MESH)

        tell(self.dev(ACROSS))
        tell(self.dev(CORE))
        tell(dict(section=1 - lax.axis_index(SECTION)))

        @pl.when(self.z < self.zs - 1)
        def _():
            tell(self.dev(UP))

        @pl.when(self.z > 0)
        def _():
            tell(self.dev(DOWN))

        ends = jnp.where(self.z < self.zs - 1, 1, 0) + jnp.where(self.z > 0, 1, 0)
        pl.semaphore_wait(sem, 3 + ends)


def part(ref, index, count):
    return ref.at[pl.ds(pl.multiple_of(index * count, 16), count), :]


def remote(src, dst, send, recv, device):
    return pltpu.make_async_remote_copy(
        src_ref=src,
        dst_ref=dst,
        send_sem=send,
        recv_sem=recv,
        device_id=device,
        device_id_type=pl.DeviceIdType.MESH,
    )


class Gather:
    def __init__(self, links, pieces, line_send, core_send, recv):
        self.k, self.pieces = links, pieces
        self.line_send, self.core_send, self.recv = line_send, core_send, recv

    def copy(self, p, z, x, c, route):
        whole, count = self.pieces[p][:2]
        ref = part(whole, self.k.owner(z, x, c), count)
        if route == CORE:
            send = self.core_send.at[p, 2 * z + x]
        else:
            send = self.line_send.at[p, route, z]
        return remote(ref, ref, send, self.recv.at[p, self.k.owner(z, x, c)], self.k.dev(route))

    def each(self, p, side, r, act):
        k = self.k
        lo, hi = self.pieces[p][2:]
        z = k.z - r if side == BELOW else k.z + r

        @pl.when((z >= lo) & (z < hi))
        def _():
            act(z)

    def pump(self, ps, do):
        k = self.k
        for r in range(k.zs):
            for p in ps:

                def out(z, p=p, r=r, side=None):
                    def go(route):
                        copy = self.copy(p, z, k.x, k.c, route)
                        copy.wait_send() if do == FINISH else copy.start()

                    if r and do == FORWARD:
                        self.copy(p, z, k.x, k.c, ACROSS).wait_recv()
                    if side != ABOVE:

                        @pl.when(k.z < k.zs - 1)
                        def _():
                            go(UP)

                    if side != BELOW:

                        @pl.when(k.z > 0)
                        def _():
                            go(DOWN)

                    go(ACROSS)
                    go(CORE)

                if r == 0:
                    if do != FORWARD:
                        self.each(p, BELOW, 0, out)
                elif do != START:
                    self.each(p, BELOW, r, functools.partial(out, side=BELOW))
                    self.each(p, ABOVE, r, functools.partial(out, side=ABOVE))
            if do == START:
                continue
            for p in ps:

                def across(z, p=p):
                    copy = self.copy(p, z, 1 - k.x, k.c, CORE)
                    if do == FINISH:
                        copy.wait_send()
                    else:
                        copy.wait_recv()
                        copy.start()

                self.each(p, BELOW, r, across)
                if r:
                    self.each(p, ABOVE, r, across)
        if do == FORWARD:
            for p in ps:
                for z in range(*self.pieces[p][2:]):
                    for x in range(2):
                        self.copy(p, z, x, 1 - k.c, CORE).wait_recv()


def add_rows(dst, src, count):
    step = 48 if count % 48 == 0 else 16

    def add(i, carry):
        s = pl.ds(pl.multiple_of(i * step, 16), step)
        dst[s, :] = (dst[s, :].astype(f32) + src[s, :].astype(f32)).astype(dst.dtype)
        return carry

    lax.fori_loop(0, count // step, add, 0)


class Scatter:
    def __init__(self, links, pieces, core_sems, line_sems):
        self.k, self.pieces = links, pieces
        self.core_sems, self.line_sems = core_sems, line_sems

    def copy(self, p, route, z, x=None):
        k = self.k
        g, core, across, below, above, _, count = self.pieces[p]
        if route == CORE:
            slot = 2 * z + x
            send, recv = self.core_sems.at[p, 0, slot], self.core_sems.at[p, 1, slot]
            src, dst = part(g, k.owner(z, x, 1 - k.c), count), part(core, slot, count)
        else:
            at = route
            send, recv = self.line_sems.at[p, 2 * at, z], self.line_sems.at[p, 2 * at + 1, z]
            src = part(g, k.owner(z, 1 - k.x if route == ACROSS else k.x, k.c), count)
            dst = part((below, above, across)[at], z, count)
        return remote(src, dst, send, recv, k.dev(route))

    def far_first(self, i):
        k = self.k
        table = [sorted(range(k.zs), key=lambda o: (-abs(o - z), o))[i] for z in range(k.zs)]
        z = table[0]
        for at in range(1, k.zs):
            z = jnp.where(k.z == at, table[at], z)
        return z

    def start(self, p):
        for i in range(self.k.zs):
            z = self.far_first(i)
            for x in (1 - self.k.x, self.k.x):
                self.copy(p, CORE, z, x).start()

    def across(self, p):
        k = self.k
        g, core, count = self.pieces[p][0], self.pieces[p][1], self.pieces[p][6]
        for i in range(k.zs):
            z = self.far_first(i)
            for x in (1 - k.x, k.x):
                self.copy(p, CORE, z, x).wait_recv()
                add_rows(part(g, k.owner(z, x, k.c), count), part(core, 2 * z + x, count), count)
                if x is not k.x:
                    self.copy(p, ACROSS, z).start()

    def line(self, p):
        k = self.k
        g, _, across, below, above, result, count = self.pieces[p]
        for i in range(k.zs):
            z = self.far_first(i)
            mine = part(g, k.owner(z, k.x, k.c), count)
            self.copy(p, ACROSS, z).wait_recv()
            add_rows(mine, part(across, z, count), count)

            def hop(route, inner, source):
                @pl.when(inner)
                def _():
                    self.copy(p, route, z).wait_recv()
                    add_rows(mine, part(source, z, count), count)

                self.copy(p, route, z).start()

            @pl.when(z > k.z)
            def _():
                hop(UP, k.z > 0, below)

            @pl.when(z < k.z)
            def _():
                hop(DOWN, k.z < k.zs - 1, above)

            @pl.when(z == k.z)
            def _():
                result[...] = mine[...].astype(f32)

                @pl.when(k.z > 0)
                def _():
                    self.copy(p, UP, z).wait_recv()
                    add_rows(result, part(below, z, count), count)

                @pl.when(k.z < k.zs - 1)
                def _():
                    self.copy(p, DOWN, z).wait_recv()
                    add_rows(result, part(above, z, count), count)

    def finish(self, p):
        k = self.k
        for z in range(k.zs):
            for x in range(2):
                self.copy(p, CORE, z, x).wait_send()
            self.copy(p, ACROSS, z).wait_send()

            @pl.when(z > k.z)
            def _():
                self.copy(p, UP, z).wait_send()

            @pl.when(z < k.z)
            def _():
                self.copy(p, DOWN, z).wait_send()


def block(names, inside, n, *refs):
    r = types.SimpleNamespace(**dict(zip(names, refs)))
    sec = lax.axis_index(SECTION)
    links = Links(n)
    r1, r2 = 2 * DI // n, DI // n
    U, GO = r.u, r.go

    @pl.when(sec == 0)
    def _():
        for m in range(MICRO):
            U[pl.ds(m * T, T), :] = r.inputs[m]

    @pl.when(sec == 1)
    def _():
        for m in range(MICRO):
            GO[pl.ds(m * T, T), :] = r.cotangent[m]

    if inside:
        for whole, shard, count in (
            (r.win, r.win_shard, r1),
            (r.wout, r.wout_shard, r2),
            (r.small, r.small_shard, r2),
        ):
            part(whole, links.i, count)[...] = shard[...]
        links.barrier()
        half = links.zs // 2
        gather = Gather(
            links,
            [
                (r.small, r2, 0, links.zs),
                (r.win, r1, 0, half),
                (r.win, r1, half, links.zs),
                (r.wout, r2, 0, links.zs),
            ],
            r.ag_line,
            r.ag_core,
            r.ag_recv,
        )
        gather.pump((0, 1, 2, 3), START)
        gather.pump((0, 1), FORWARD)

        @pl.when(sec == 1)
        def _():
            gather.pump((2, 3), FORWARD)
    else:
        sem = pltpu.get_barrier_semaphore()
        pl.semaphore_signal(
            sem, inc=1, device_id=dict(section=1 - sec), device_id_type=pl.DeviceIdType.MESH
        )
        pl.semaphore_wait(sem, 1)

    rows, small, gain, win, wout = r.rows, r.small, r.gain, r.win, r.wout
    for c in range(DI // C):
        s = pl.ds(c * C, C)
        tr = small[s, 128:256].astype(f32).T
        rows[0:NS, s] = -jnp.exp(tr[0:NS]) * LOG2E
        rows[NS : NS + 8, s] = tr[NS : NS + 8]
    if inside:
        gw = D // n
        lane = iota((1, D), 1)
        acc = jnp.zeros((1, D), f32)
        for i in range(n):
            piece = small[i * r2 : i * r2 + 16, 128:256].astype(f32)[0:1]
            spread = jnp.concatenate([piece, jnp.zeros((1, D - 128), f32)], axis=1)
            moved = pltpu.roll(spread, (i * gw - GAIN_LANE) % D, 1)
            acc = jnp.where((lane >= i * gw) & (lane < (i + 1) * gw), moved, acc)
        gain[...] = acc

    def of(ref, m):
        return ref.at[pl.ds(pl.multiple_of(m * T, T), T), :]

    def boundary(route, m):
        if route == RIGHT:
            src, dst, at = r.section_out.at[m], of(r.u, m), 0
        else:
            src, dst, at = of(r.back, m), of(r.go, m), 1
        return remote(src, dst, r.edge.at[at, 0, m], r.edge.at[at, 1, m], dict(section=1 - sec))

    def forward(k, carry):
        m = k - sec

        @pl.when((m >= 0) & (m < MICRO))
        def _():
            @pl.when(sec == 1)
            def _():
                boundary(RIGHT, m).wait_recv()

            u = of(r.u, m)
            reset = r.reset[m]
            v = u[...].astype(f32)
            inv = lax.rsqrt(jnp.mean(v * v, axis=-1, keepdims=True) + EPS)
            of(r.normed, m)[...] = (v * inv * gain[...]).astype(bf16)
            f_x(reset, of(r.normed, m), win, rows, of(r.x, m), of(r.act, m))
            f_rate(
                reset,
                of(r.act, m),
                small,
                rows,
                of(r.proj, m),
                of(r.rin, m),
                of(r.pre, m),
                r.dec,
                r.gs,
                r.cols,
                r.diag,
            )
            f_scan(
                of(r.act, m), rows, r.dec, r.gs, r.cols, r.diag, r.h.at[m], of(r.ssm, m)
            )
            if inside:

                @pl.when((sec == 0) & (m == 0))
                def _():
                    gather.pump((2, 3), FORWARD)

            f_out(
                u, of(r.normed, m), win, wout, of(r.ssm, m), of(r.z, m), of(r.gated, m), r.section_out.at[m]
            )

            @pl.when(sec == 0)
            def _():
                boundary(RIGHT, m).start()

        return carry

    lax.fori_loop(0, MICRO + 1, forward, 0)
    if inside:
        gather.pump((0, 1, 2, 3), FINISH)

    def backward(k, carry):
        m = k - (1 - sec)

        @pl.when((m >= 0) & (m < MICRO))
        def _():
            @pl.when(sec == 0)
            def _():
                boundary(LEFT, m).wait_recv()

            first = m == 0
            reset = r.reset[m]
            go, gm, sm = of(r.go, m), of(r.gm, m), r.sm
            act, pre = of(r.act, m), of(r.pre, m)
            gs, gd, gr, gb, gc = r.gs, r.dec, r.gr, r.gb, r.gc
            b_gate(first, go, wout, of(r.z, m), of(r.ssm, m), act, gs, gm, sm)
            b_prep(reset, pre, act, of(r.proj, m), r.dec, r.drive, r.cols, r.diag)
            b_scan(
                first,
                gs,
                rows,
                r.dec,
                r.cols,
                r.diag,
                r.drive,
                r.h.at[m],
                r.adj,
                gd,
                gr,
                gb,
                gc,
                sm,
            )
            b_pre(first, act, pre, small, gd, gr, gb, gc, of(r.gpre, m), of(r.gp, m), sm)
            b_conv(first, reset, rows, small, of(r.x, m), gs, gd, pre, of(r.gp, m), gm, sm)
            sg = r.section_grad.at[m]
            b_in(first, of(r.u, m), go, gain, win, gm, sg, r.gg)

            @pl.when(sec == 1)
            def _():
                of(r.back, m)[...] = sg[...].astype(bf16)
                boundary(LEFT, m).start()

        return carry

    lax.fori_loop(0, MICRO + 1, backward, 0)

    gwi, gwo, gws = r.gwi, r.gwo, r.gws
    for c in range(DI // C):
        s = pl.ds(c * C, C)
        gwo[s, :] = tn(r.gated[:, s], GO[...]).astype(gwo.dtype)
    for c in range(2 * DI // C):
        s = pl.ds(c * C, C)
        gwi[s, :] = tn(r.gm[:, s], r.normed[...]).astype(gwi.dtype)
    for c in range(DI // C):
        s = pl.ds(c * C, C)
        head = tn(r.act[:, s], r.gp[...]) + tn(r.gpre[:, s], r.rin[...])
        gws[s, 0:128] = head.astype(gws.dtype)
        tail = jnp.concatenate([r.sm[0:24, s], jnp.zeros((104, C), f32)], axis=0).T
        gws[s, 128:256] = tail.astype(gws.dtype)
    if inside:
        lane = iota((16, 128), 1)
        own = (iota((16, 128), 0) == 0) & (lane >= GAIN_LANE) & (lane < GAIN_LANE + gw)
        for i in range(n):
            moved = pltpu.roll(r.gg[...], (GAIN_LANE - i * gw) % D, 1)[:, 0:128]
            at = pl.ds(i * r2, 16)
            old = gws[at, 128:256].astype(f32)
            gws[at, 128:256] = jnp.where(own, jnp.broadcast_to(moved, (16, 128)), old).astype(gws.dtype)
        scatter = Scatter(
            links,
            [
                (gwo, r.co, r.xo, r.uo, r.do, r.gout_shard, r2),
                (gwi, r.ci, r.xi, r.ui, r.di, r.gin_shard, r1),
                (gws, r.cs, r.xs, r.us, r.ds, r.gsmall_shard, r2),
            ],
            r.rs_core,
            r.rs_line,
        )
        for stage in (scatter.start, scatter.across, scatter.line, scatter.finish):
            for p in range(3):
                stage(p)

    for m in range(MICRO):

        @pl.when(sec == 0)
        def _():
            boundary(RIGHT, m).wait_send()

        @pl.when(sec == 1)
        def _():
            boundary(LEFT, m).wait_send()


def call(n, inside, arrays):
    r1, r2, zs = 2 * DI // n, DI // n, n // 4
    rows2 = MICRO * T
    outs = dict(
        section_out=((MICRO, T, D), bf16),
        section_grad=((MICRO, T, D), f32),
    )
    scratch = dict(
        u=((rows2, D), bf16),
        go=((rows2, D), bf16),
        back=((rows2, D), bf16),
        normed=((rows2, D), bf16),
        x=((rows2, DI), f32),
        z=((rows2, DI), f32),
        pre=((rows2, DI), f32),
        ssm=((rows2, DI), f32),
        act=((rows2, DI), bf16),
        gated=((rows2, DI), bf16),
        gpre=((rows2, DI), bf16),
        gm=((rows2, 2 * DI), bf16),
        proj=((rows2, 128), f32),
        rin=((rows2, 128), bf16),
        gp=((rows2, 128), bf16),
        h=((MICRO, (T + 1) * NS, DI), bf16),
        adj=((T * NS, CS), bf16),
        dec=((T, DI), f32),
        gs=((T, DI), f32),
        gr=((T, DI), f32),
        gb=((T, NS * TB), f32),
        gc=((T, NS * TB), bf16),
        drive=((T, DI), bf16),
        cols=((T * NS, 128), f32),
        diag=((T, NS * TB), bf16),
        rows=((32, DI), f32),
        sm=((32, DI), f32),
    )
    sems = dict(edge=(2, 2, MICRO))
    if inside:
        outs |= dict(gin_shard=((r1, D), f32))
        outs |= dict(gout_shard=((r2, D), f32))
        outs |= dict(gsmall_shard=((r2, 256), f32))
        scratch |= dict(gain=((1, D), f32))
        scratch |= dict(gg=((1, D), f32))
        scratch |= dict(win=((2 * DI, D), bf16))
        scratch |= dict(wout=((DI, D), bf16))
        scratch |= dict(small=((DI, 256), bf16))
        scratch |= dict(gwi=((2 * DI, D), bf16))
        scratch |= dict(gwo=((DI, D), bf16))
        scratch |= dict(gws=((DI, 256), bf16))
        two, one = 2 * zs, zs
        scratch |= dict(ci=((two * r1, D), bf16), co=((two * r2, D), bf16), cs=((two * r2, 256), bf16))
        scratch |= dict(xi=((one * r1, D), bf16), xo=((one * r2, D), bf16), xs=((one * r2, 256), bf16))
        scratch |= dict(ui=((one * r1, D), bf16), uo=((one * r2, D), bf16), us=((one * r2, 256), bf16))
        scratch |= dict(di=((one * r1, D), bf16), do=((one * r2, D), bf16), ds=((one * r2, 256), bf16))
        sems |= dict(ag_line=(4, 3, zs))
        sems |= dict(ag_core=(4, 2 * zs))
        sems |= dict(ag_recv=(4, n))
        sems |= dict(rs_core=(3, 2, 2 * zs))
        sems |= dict(rs_line=(3, 6, zs))
    else:
        outs |= dict(gwi=((2 * DI, D), f32))
        outs |= dict(gwo=((DI, D), f32))
        outs |= dict(gws=((DI, 256), f32))
        outs |= dict(gg=((1, D), f32))
    names = list(arrays) + list(outs) + list(scratch) + list(sems)
    whole = pl.BlockSpec(memory_space=pltpu.VMEM)
    results = pl.pallas_call(
        functools.partial(block, names, inside, n),
        out_shape=[jax.ShapeDtypeStruct(*spec) for spec in outs.values()],
        in_specs=[whole] * len(arrays),
        out_specs=[whole] * len(outs),
        scratch_shapes=[pltpu.VMEM(*spec) for spec in scratch.values()]
        + [pltpu.SemaphoreType.DMA(shape) for shape in sems.values()],
        compiler_params=pltpu.CompilerParams(
            collective_id=0, has_side_effects=True, vmem_limit_bytes=63 * 2**20
        ),
        name="two_layer_block",
    )(*arrays.values())
    return types.SimpleNamespace(**dict(zip(outs, results)))


def on_device(
    inputs,
    cotangent,
    markers,
    norm_gain,
    in_proj,
    conv_weight,
    conv_bias,
    x_proj,
    dt_proj,
    dt_bias,
    a_log,
    d_skip,
    out_proj,
):
    n = lax.axis_size(DP)
    inside = n % 4 == 0 and (DI // n) % 16 == 0
    r2, gw = DI // n, D // n
    first = (jnp.arange(T) == 0)[None, :]
    reset = jnp.where((markers > 0) | first, 1.0, 0.0).astype(f32)[:, :, None]
    win = in_proj[0].T.astype(bf16)
    wout = out_proj[0].astype(bf16)
    gain = jnp.zeros((r2, 128 - GAIN_LANE), f32).at[0, 0:gw].set(norm_gain[0])
    small = jnp.concatenate(
        [
            x_proj[0],
            dt_proj[0].T,
            a_log[0],
            conv_weight[0].T,
            conv_bias[0][:, None],
            dt_bias[0][:, None],
            d_skip[0][:, None],
            jnp.zeros((r2, 1), f32),
            gain,
        ],
        axis=1,
    ).astype(bf16)
    arrays = dict(inputs=inputs, cotangent=cotangent, reset=reset)
    if inside:
        arrays |= dict(win_shard=win, wout_shard=wout, small_shard=small)
        res = call(n, inside, arrays)
        gin, gout, gsmall = res.gin_shard, res.gout_shard, res.gsmall_shard
        ggain = gsmall[0, 128 + GAIN_LANE : 128 + GAIN_LANE + gw]
    else:
        gains = lax.all_gather(norm_gain.astype(bf16), DP, axis=1, tiled=True).astype(f32)
        arrays |= dict(
            win=lax.all_gather(win, DP, axis=0, tiled=True),
            wout=lax.all_gather(wout, DP, axis=0, tiled=True),
            small=lax.all_gather(small, DP, axis=0, tiled=True),
            gain=gains,
        )
        res = call(n, inside, arrays)
        gin = lax.psum_scatter(res.gwi, DP, scatter_dimension=0, tiled=True)
        gout = lax.psum_scatter(res.gwo, DP, scatter_dimension=0, tiled=True)
        gsmall = lax.psum_scatter(res.gws, DP, scatter_dimension=0, tiled=True)
        ggain = lax.psum_scatter(res.gg, DP, scatter_dimension=1, tiled=True)[0]
    tail = gsmall[:, 128:]
    return (
        res.section_out[None],
        res.section_grad[None],
        ggain[None],
        gin.T[None],
        tail[:, NS : NS + KC].T[None],
        tail[:, 20][None],
        gsmall[:, 0 : RK + 2 * NS][None],
        gsmall[:, RK + 2 * NS : 128].T[None],
        tail[:, 21][None],
        tail[:, 0:NS][None],
        tail[:, 22][None],
        gout[None],
    )


def solution(mesh):
    tokens = P(None, DP, None)
    columns = P(SECTION, None, DP)
    channels = P(SECTION, DP)
    rows = P(SECTION, DP, None)
    kept = P(SECTION, None, DP, None)
    weights = (
        channels,
        columns,
        columns,
        channels,
        rows,
        columns,
        channels,
        rows,
        channels,
        rows,
    )
    return jax.shard_map(
        on_device,
        mesh=mesh,
        in_specs=(tokens, tokens, P(None, DP)) + weights,
        out_specs=(kept, kept) + weights,
        check_vma=False,
    )
```

time: 5380 us -> 224 us (0.04); the launches traced: 5310 us -> 224 us
  local copies, waits for them, and re-layouts: 2170 us -> 12.2 us
  waiting for transfers between devices: 2040 us -> 0 us
  other arithmetic: 858 us -> 2.56 us
  Pallas kernels: 0 us -> 208 us
  blocking collectives: 149 us -> 0 us
  matrix products: 57.3 us -> 0 us
    pad x144 -> x0, local copies, waits for them, and re-layouts: 1860 us -> none  [the longest x96 1230 us: block_step(): lax.associative_scan(combine, (decay_factor, drive_term), axis=0)]
    ppermute x4 -> x0, waiting for transfers between devices: 1430 us -> none  [shifted(): lax.ppermute(value, axis, [(source, source + steps) for source in range(i...]
    unnamed x20 -> x0, waiting for transfers between devices: 414 us -> none
    mul x88 -> x0, other arithmetic: 321 us -> none  [the longest x72 284 us: combine(): return (earlier[0] * following[0], following[0] * earlier[1] + following[1])]
    add x76 -> x0, other arithmetic: 210 us -> none  [the longest x46 106 us: block_step(): lax.associative_scan(combine, (decay_factor, drive_term), axis=0)]
    pallas_call x0 -> x1, Pallas kernels: none -> 208 us  [call(): pl.pallas_call(functools.partial(block, names, inside, n), out_shape=[jax...]
    reduce_scatter x2 -> x0, waiting for transfers between devices: 193 us -> none  [the longest x1 116 us: on_device(): lax.psum_scatter(totals[1][None], 'dp', scatter_dimension=2, tiled=True)]
    slice x116 -> x2, local copies, waits for them, and re-layouts: 160 us -> 2.3 us  [the longest x1 1.72 us: on_device(): tail[:, 22][None]]
  transfers between devices with their start and end apart: 16 -> 0, of which waited for: 12 -> 0; matrix products, arithmetic and copies ran while one was open for 2% -> 0% of each run, Pallas kernels for 0% -> 0%
where the time goes in v1:
time: 224 us
  Pallas kernels  208 us (93%)
  local copies, waits for them, and re-layouts  12.2 us (5%)
  other arithmetic  2.56 us (1%)
    pallas_call x1, Pallas kernels, call(): pl.pallas_call(functools.partial(block, names, inside, n), out_shape=[jax...  208 us
    unnamed x42, local copies, waits for them, and re-layouts  7.8 us

profile of v1, /device:TPU:0, one launch (start us, length us, event | category | flops | bytes accessed | tf_op | source)
XLA Modules:
  0.0 223.9 jit_solution(10268888965519259592)
XLA Ops:
  0.6 0.0 copy-start.11
  0.7 0.0 copy-start.12
  0.7 0.0 copy-start.13
  0.7 0.0 copy-start.14
  0.7 0.0 copy-start.9
  0.7 0.0 copy-start.8
  0.7 0.0 copy-start.7
  0.7 0.0 copy-start.6
  0.7 1.9 convert_bitcast_fusion.refs_3_
  2.6 0.0 copy-done.11
  2.6 0.0 copy-start.4
  2.6 0.1 copy.40
  2.7 0.0 copy-done.12
  2.7 0.1 copy.41
  2.9 0.0 copy-done.13
  2.9 0.1 copy.42
  3.0 0.0 copy-done.14
  3.0 0.0 copy-done.9
  3.0 0.1 copy.39
  3.1 0.0 copy-done.8
  3.2 0.1 copy.38
  3.3 0.0 copy-done.7
  3.3 0.1 copy.37
  3.4 0.0 copy-done.6
  3.4 0.1 copy.36
  3.5 0.8 concatenate.6.refs_5_
  4.2 0.0 copy-done.4
  4.2 0.7 convert_bitcast_fusion.1.refs_4_
  4.9 0.0 copy-start.10
  4.9 0.7 copy-done.10
  5.6 0.8 copy.43.refs_2_
  6.4 208.3 %two_layer_block.1 = (bf16[2,128,768]{2,1,0:T(8,128)(2,1)}, f32[2,128,768]{2,1,0:T(8,128)}, f32[192,768]{1,0:T(8,128)}, f32[96,768]{1,0:T(8,128)}, f32[96,256]{1,0:T(8,128)}) custom-call(bf16[2,128,768]{2,1,0:T(8,128)(2,1)} %refs_0_.1, bf16[2,128,768]{2,1,0:T(8,128)(2,1)} %refs_1_.1, f32[2,128,1]{2,1,0:T(8,128)} %copy.43.refs_2_, ...), custom_call_target="tpu_custom_call" | custom-call | tf_op jit(solution)/shard_map/two_layer_block/pallas_call | solution.py:814
  214.7 0.0 copy-start
  214.7 0.0 copy-start.3
  214.7 0.0 copy-start.1
  214.7 1.7 slice_reduce_fusion
  216.5 0.0 copy-done
  216.5 0.7 copy.45
  217.2 0.1 slice_bitcast_fusion.1
  217.2 0.7 copy.46
  217.9 0.7 copy.47
  218.6 0.1 slice_bitcast_fusion.3
  218.7 0.7 copy.44
  219.3 0.6 slice.46
  219.9 0.0 copy-done.3
  219.9 0.7 copy.52
  220.7 0.0 copy-done.1
  220.7 0.0 copy-start.2
  220.7 0.9 copy.53
  221.6 0.5 copy-done.2
  222.0 0.0 copy-start.5
  222.0 0.8 copy.54
  222.8 0.3 copy-done.5
  223.2 0.7 copy.55
  (10 shorter events, 0.0 us)
Async XLA Ops:
  0.6 1.9 copy-start.11
  0.7 2.1 copy-start.12
  0.7 2.2 copy-start.13
  0.7 2.3 %copy-start.14 = (f32[1,48]{1,0:T(1,128)S(1)}, f32[1,48]{1,0:T(1,128)}, u32[]{:S(2)}) copy-start(f32[1,48]{1,0:T(1,128)} %param.18) | copy-start | bytes 580
  0.7 2.3 %copy-start.9 = (f32[1,4,96]{2,1,0:T(4,128)S(1)}, f32[1,4,96]{2,1,0:T(4,128)}, u32[]{:S(2)}) copy-start(f32[1,4,96]{2,1,0:T(4,128)} %param.20) | copy-start | bytes 4612
  0.7 2.5 %copy-start.8 = (f32[1,96,16]{1,2,0:T(8,128)S(1)}, f32[1,96,16]{1,2,0:T(8,128)}, u32[]{:S(2)}) copy-start(f32[1,96,16]{1,2,0:T(8,128)} %param.25) | copy-start | bytes 18436
  0.7 2.6 %copy-start.7 = (f32[1,48,96]{2,1,0:T(8,128)S(1)}, f32[1,48,96]{2,1,0:T(8,128)}, u32[]{:S(2)}) copy-start(f32[1,48,96]{2,1,0:T(8,128)} %param.23) | copy-start | bytes 55300
  0.7 2.6 %copy-start.6 = (f32[1,96,80]{1,2,0:T(8,128)S(1)}, f32[1,96,80]{1,2,0:T(8,128)}, u32[]{:S(2)}) copy-start(f32[1,96,80]{1,2,0:T(8,128)} %param.22) | copy-start | bytes 92164
  2.6 1.7 copy-start.4
  4.9 0.7 copy-start.10
  214.7 1.7 copy-start
  214.7 5.2 %copy-start.3 = (bf16[2,128,768]{2,1,0:T(8,128)(2,1)S(1)}, bf16[2,128,768]{2,1,0:T(8,128)(2,1)}, u32[]{:S(2)}) copy-start(bf16[2,128,768]{2,1,0:T(8,128)(2,1)} %get-tuple-element.29) | copy-start | bytes 1179652
  214.7 6.0 %copy-start.1 = (f32[2,128,768]{2,1,0:T(8,128)S(1)}, f32[2,128,768]{2,1,0:T(8,128)}, u32[]{:S(2)}) copy-start(f32[2,128,768]{2,1,0:T(8,128)} %get-tuple-element.30) | copy-start | bytes 2359300
  220.7 1.3 copy-start.2
  222.0 1.1 copy-start.5

commit v2 on v1

--- a/solution.py
+++ b/solution.py
@@ -23,11 +23,10 @@
 LOG2E = 1.4426950408889634
 LN2 = 0.6931471805599453
 BIG = 1e30
-GAIN_LANE = 24
 DP, SECTION = "dp", "section"
 UP, DOWN, ACROSS, CORE = range(4)
 BELOW, ABOVE = range(2)
-START, FORWARD, FINISH = range(3)
+START, FINISH = range(2)
 RIGHT, LEFT = range(2)
 f32 = jnp.float32
 bf16 = jnp.bfloat16
@@ -299,7 +298,7 @@
         step = (4, -4, 2 - 4 * self.x, 1 - 2 * self.c)[route]
         return dict(dp=self.i + step)
 
-    def barrier(self):
+    def greet(self):
         sem = pltpu.get_barrier_semaphore()
 
         def tell(device):
@@ -317,8 +316,9 @@
         def _():
             tell(self.dev(DOWN))
 
+    def meet(self):
         ends = jnp.where(self.z < self.zs - 1, 1, 0) + jnp.where(self.z > 0, 1, 0)
-        pl.semaphore_wait(sem, 3 + ends)
+        pl.semaphore_wait(pltpu.get_barrier_semaphore(), 3 + ends)
 
 
 def part(ref, index, count):
@@ -359,59 +359,65 @@
         def _():
             act(z)
 
-    def pump(self, ps, do):
+    def line(self, p, r):
+        def pass_on(z, side):
+            k = self.k
+            self.copy(p, z, k.x, k.c, ACROSS).wait_recv()
+            self.go(p, z, side, START)
+
+        for side in (BELOW, ABOVE):
+            self.each(p, side, r, functools.partial(pass_on, side=side))
+
+    def go(self, p, z, side, do):
         k = self.k
+
+        def one(route):
+            copy = self.copy(p, z, k.x, k.c, route)
+            copy.wait_send() if do == FINISH else copy.start()
+
+        one(ACROSS)
+        if side != ABOVE:
+
+            @pl.when(k.z < k.zs - 1)
+            def _():
+                one(UP)
+
+        if side != BELOW:
+
+            @pl.when(k.z > 0)
+            def _():
+                one(DOWN)
+
+        one(CORE)
+
+    def start(self, p):
+        self.each(p, BELOW, 0, lambda z: self.go(p, z, None, START))
+
+    def across(self, p, r):
+        def pass_on(z):
+            copy = self.copy(p, z, 1 - self.k.x, self.k.c, CORE)
+            copy.wait_recv()
+            copy.start()
+
+        self.each(p, BELOW, r, pass_on)
+        if r:
+            self.each(p, ABOVE, r, pass_on)
+
+    def arrived(self, p):
+        for z in range(*self.pieces[p][2:]):
+            for x in range(2):
+                self.copy(p, z, x, 1 - self.k.c, CORE).wait_recv()
+
+    def finish(self, p):
+        k = self.k
+
+        def crossed(z):
+            self.copy(p, z, 1 - k.x, k.c, CORE).wait_send()
+
         for r in range(k.zs):
-            for p in ps:
-
-                def out(z, p=p, r=r, side=None):
-                    def go(route):
-                        copy = self.copy(p, z, k.x, k.c, route)
-                        copy.wait_send() if do == FINISH else copy.start()
-
-                    if r and do == FORWARD:
-                        self.copy(p, z, k.x, k.c, ACROSS).wait_recv()
-                    if side != ABOVE:
-
-                        @pl.when(k.z < k.zs - 1)
-                        def _():
-                            go(UP)
-
-                    if side != BELOW:
-
-                        @pl.when(k.z > 0)
-                        def _():
-                            go(DOWN)
-
-                    go(ACROSS)
-                    go(CORE)
-
-                if r == 0:
-                    if do != FORWARD:
-                        self.each(p, BELOW, 0, out)
-                elif do != START:
-                    self.each(p, BELOW, r, functools.partial(out, side=BELOW))
-                    self.each(p, ABOVE, r, functools.partial(out, side=ABOVE))
-            if do == START:
-                continue
-            for p in ps:
-
-                def across(z, p=p):
-                    copy = self.copy(p, z, 1 - k.x, k.c, CORE)
-                    if do == FINISH:
-                        copy.wait_send()
-                    else:
-                        copy.wait_recv()
-                        copy.start()
-
-                self.each(p, BELOW, r, across)
-                if r:
-                    self.each(p, ABOVE, r, across)
-        if do == FORWARD:
-            for p in ps:
-                for z in range(*self.pieces[p][2:]):
-                    for x in range(2):
-                        self.copy(p, z, x, 1 - k.c, CORE).wait_recv()
+            for side in (BELOW, ABOVE) if r else (BELOW,):
+                self.each(p, side, r, lambda z, side=side: self.go(p, z, side if r else None, FINISH))
+                self.each(p, side, r, crossed)
 
 
 def add_rows(dst, src, count):
@@ -432,37 +438,36 @@
 
     def copy(self, p, route, z, x=None):
         k = self.k
-        g, core, across, below, above, _, count = self.pieces[p]
+        g, core, across, below, above, _, count, _, _ = self.pieces[p]
         if route == CORE:
             slot = 2 * z + x
             send, recv = self.core_sems.at[p, 0, slot], self.core_sems.at[p, 1, slot]
             src, dst = part(g, k.owner(z, x, 1 - k.c), count), part(core, slot, count)
         else:
-            at = route
-            send, recv = self.line_sems.at[p, 2 * at, z], self.line_sems.at[p, 2 * at + 1, z]
+            send, recv = self.line_sems.at[p, 2 * route, z], self.line_sems.at[p, 2 * route + 1, z]
             src = part(g, k.owner(z, 1 - k.x if route == ACROSS else k.x, k.c), count)
-            dst = part((below, above, across)[at], z, count)
+            dst = part((below, above, across)[route], z, count)
         return remote(src, dst, send, recv, k.dev(route))
 
-    def far_first(self, i):
+    def far_first(self, p):
         k = self.k
-        table = [sorted(range(k.zs), key=lambda o: (-abs(o - z), o))[i] for z in range(k.zs)]
-        z = table[0]
-        for at in range(1, k.zs):
-            z = jnp.where(k.z == at, table[at], z)
-        return z
+        lo, hi = self.pieces[p][7:]
+        for i in range(hi - lo):
+            table = [sorted(range(lo, hi), key=lambda o: (-abs(o - z), o))[i] for z in range(k.zs)]
+            z = table[0]
+            for at in range(1, k.zs):
+                z = jnp.where(k.z == at, table[at], z)
+            yield z
 
     def start(self, p):
-        for i in range(self.k.zs):
-            z = self.far_first(i)
+        for z in self.far_first(p):
             for x in (1 - self.k.x, self.k.x):
                 self.copy(p, CORE, z, x).start()
 
     def across(self, p):
         k = self.k
         g, core, count = self.pieces[p][0], self.pieces[p][1], self.pieces[p][6]
-        for i in range(k.zs):
-            z = self.far_first(i)
+        for z in self.far_first(p):
             for x in (1 - k.x, k.x):
                 self.copy(p, CORE, z, x).wait_recv()
                 add_rows(part(g, k.owner(z, x, k.c), count), part(core, 2 * z + x, count), count)
@@ -471,9 +476,8 @@
 
     def line(self, p):
         k = self.k
-        g, _, across, below, above, result, count = self.pieces[p]
-        for i in range(k.zs):
-            z = self.far_first(i)
+        g, _, across, below, above, _, count, _, _ = self.pieces[p]
+        for z in self.far_first(p):
             mine = part(g, k.owner(z, k.x, k.c), count)
             self.copy(p, ACROSS, z).wait_recv()
             add_rows(mine, part(across, z, count), count)
@@ -494,23 +498,27 @@
             def _():
                 hop(DOWN, k.z < k.zs - 1, above)
 
-            @pl.when(z == k.z)
-            def _():
-                result[...] = mine[...].astype(f32)
-
-                @pl.when(k.z > 0)
-                def _():
-                    self.copy(p, UP, z).wait_recv()
-                    add_rows(result, part(below, z, count), count)
-
-                @pl.when(k.z < k.zs - 1)
-                def _():
-                    self.copy(p, DOWN, z).wait_recv()
-                    add_rows(result, part(above, z, count), count)
+    def own(self, p):
+        k = self.k
+        g, _, _, below, above, result, count, lo, hi = self.pieces[p]
+
+        @pl.when((k.z >= lo) & (k.z < hi))
+        def _():
+            result[...] = part(g, k.i, count)[...].astype(f32)
+
+            @pl.when(k.z > 0)
+            def _():
+                self.copy(p, UP, k.z).wait_recv()
+                add_rows(result, part(below, k.z, count), count)
+
+            @pl.when(k.z < k.zs - 1)
+            def _():
+                self.copy(p, DOWN, k.z).wait_recv()
+                add_rows(result, part(above, k.z, count), count)
 
     def finish(self, p):
         k = self.k
-        for z in range(k.zs):
+        for z in range(*self.pieces[p][7:]):
             for x in range(2):
                 self.copy(p, CORE, z, x).wait_send()
             self.copy(p, ACROSS, z).wait_send()
@@ -522,85 +530,120 @@
             @pl.when(z < k.z)
             def _():
                 self.copy(p, DOWN, z).wait_send()
+
+
+def weight_rows(tails, rows, gain, n):
+    r2, gw = DI // n, D // n
+    parts = [tails[i * 32 : i * 32 + 32, :].astype(f32) for i in range(n)]
+    rows[...] = jnp.concatenate([p[:, 0:r2] for p in parts], axis=1)
+    gain[...] = jnp.concatenate([p[23:24, 0:gw] for p in parts], axis=1)
 
 
 def block(names, inside, n, *refs):
     r = types.SimpleNamespace(**dict(zip(names, refs)))
     sec = lax.axis_index(SECTION)
     links = Links(n)
-    r1, r2 = 2 * DI // n, DI // n
-    U, GO = r.u, r.go
-
-    @pl.when(sec == 0)
-    def _():
-        for m in range(MICRO):
-            U[pl.ds(m * T, T), :] = r.inputs[m]
-
-    @pl.when(sec == 1)
-    def _():
-        for m in range(MICRO):
-            GO[pl.ds(m * T, T), :] = r.cotangent[m]
+    r1, r2, gw = 2 * DI // n, DI // n, D // n
+    rows, small, gain, win, wout = r.rows, r.small, r.gain, r.win, r.wout
+
+    def of(ref, m):
+        return ref.at[pl.ds(pl.multiple_of(m * T, T), T), :]
+
+    def load(m, at):
+        src, dst = ((r.inputs, r.u), (r.cotangent, r.go))[at]
+        return pltpu.make_async_copy(src.at[m], of(dst, m), r.loads.at[m])
+
+    r.sm[...] = jnp.zeros_like(r.sm)
+    starts = jnp.where((r.markers[...] > 0) | (iota((MICRO, T), 1) == 0), 1.0, 0.0)
+    starts = jnp.concatenate([starts, jnp.zeros((8 - MICRO, T), f32)], axis=0).T
+    for m in range(MICRO):
+        r.reset[m] = jnp.broadcast_to(starts[:, m : m + 1], (T, 128))
+    for at in range(2):
+
+        @pl.when(sec == at)
+        def _():
+            for m in range(MICRO):
+                load(m, at).start()
+
+    def boundary(route, m):
+        if route == RIGHT:
+            src, dst, at = r.section_out.at[m], of(r.u, m), 0
+        else:
+            src, dst, at = of(r.back, m), of(r.go, m), 1
+        return remote(src, dst, r.edge.at[at, 0, m], r.edge.at[at, 1, m], dict(section=1 - sec))
 
     if inside:
-        for whole, shard, count in (
-            (r.win, r.win_shard, r1),
-            (r.wout, r.wout_shard, r2),
-            (r.small, r.small_shard, r2),
-        ):
-            part(whole, links.i, count)[...] = shard[...]
-        links.barrier()
+        tails = r.tails
+        links.greet()
+        part(win, links.i, r1)[...] = r.in_proj[...].astype(bf16)
+        part(wout, links.i, r2)[...] = r.out_proj[0].astype(bf16)
+        head = jnp.concatenate([r.x_proj[...], r.dt_proj[0]], axis=0).T
+        part(small, links.i, r2)[...] = head.astype(bf16)
+        top = [r.a_log[...], r.conv_weight[0], r.conv_bias[...], r.dt_bias[...], r.d_skip[...]]
+        top.append(jnp.concatenate([r.norm_gain[...], jnp.zeros((1, r2 - gw), f32)], axis=1))
+        top = jnp.concatenate(top + [jnp.zeros((8, r2), f32)], axis=0)
+        top = jnp.concatenate([top, jnp.zeros((32, 128 - r2), f32)], axis=1)
+        part(tails, links.i, 32)[...] = top.astype(bf16)
+        links.meet()
         half = links.zs // 2
-        gather = Gather(
+        pieces = [
+            (tails, 32, 0, links.zs),
+            (small, r2, 0, links.zs),
+            (win, r1, 0, half),
+            (win, r1, half, links.zs),
+            (wout, r2, 0, links.zs),
+        ]
+        gather = Gather(links, pieces, r.ag_line, r.ag_core, r.ag_recv)
+        early, late = (0, 1, 2), (3, 4)
+
+        def pass_on(ps, hops):
+            for hop in hops:
+                for p in ps:
+                    if hop < links.zs:
+                        gather.line(p, hop)
+                for p in ps:
+                    gather.across(p, hop - 1)
+
+        for p in early + late:
+            gather.start(p)
+        pass_on(early + late, range(1, links.zs - 1))
+        pass_on(early, range(links.zs - 1, links.zs + 1))
+        for p in early:
+            gather.arrived(p)
+
+        def rest(hops):
+            pass_on(late, hops)
+            if links.zs in hops:
+                for p in late:
+                    gather.arrived(p)
+
+        @pl.when(sec == 1)
+        def _():
+            rest((links.zs - 1, links.zs))
+
+        weight_rows(tails, rows, gain, n)
+        scatter = Scatter(
             links,
             [
-                (r.small, r2, 0, links.zs),
-                (r.win, r1, 0, half),
-                (r.win, r1, half, links.zs),
-                (r.wout, r2, 0, links.zs),
+                (r.gwo, r.co, r.xo, r.uo, r.do, r.gout_shard, r2, 0, links.zs),
+                (r.gwi, r.ci, r.xi, r.ui, r.di, r.gin_shard, r1, half, links.zs),
+                (r.gwi, r.ci, r.xi, r.ui, r.di, r.gin_shard, r1, 0, half),
+                (r.gws, r.cs, r.xs, r.us, r.ds, r.gsmall_shard, r2, 0, links.zs),
+                (r.gwt, r.ct, r.xt, r.ut, r.dt, r.gtail_shard, 32, 0, links.zs),
             ],
-            r.ag_line,
-            r.ag_core,
-            r.ag_recv,
+            r.rs_core,
+            r.rs_line,
         )
-        gather.pump((0, 1, 2, 3), START)
-        gather.pump((0, 1), FORWARD)
-
-        @pl.when(sec == 1)
-        def _():
-            gather.pump((2, 3), FORWARD)
     else:
         sem = pltpu.get_barrier_semaphore()
         pl.semaphore_signal(
             sem, inc=1, device_id=dict(section=1 - sec), device_id_type=pl.DeviceIdType.MESH
         )
         pl.semaphore_wait(sem, 1)
-
-    rows, small, gain, win, wout = r.rows, r.small, r.gain, r.win, r.wout
+        rows[...] = r.raw_rows[...]
     for c in range(DI // C):
         s = pl.ds(c * C, C)
-        tr = small[s, 128:256].astype(f32).T
-        rows[0:NS, s] = -jnp.exp(tr[0:NS]) * LOG2E
-        rows[NS : NS + 8, s] = tr[NS : NS + 8]
-    if inside:
-        gw = D // n
-        lane = iota((1, D), 1)
-        acc = jnp.zeros((1, D), f32)
-        for i in range(n):
-            piece = small[i * r2 : i * r2 + 16, 128:256].astype(f32)[0:1]
-            spread = jnp.concatenate([piece, jnp.zeros((1, D - 128), f32)], axis=1)
-            moved = pltpu.roll(spread, (i * gw - GAIN_LANE) % D, 1)
-            acc = jnp.where((lane >= i * gw) & (lane < (i + 1) * gw), moved, acc)
-        gain[...] = acc
-
-    def of(ref, m):
-        return ref.at[pl.ds(pl.multiple_of(m * T, T), T), :]
-
-    def boundary(route, m):
-        if route == RIGHT:
-            src, dst, at = r.section_out.at[m], of(r.u, m), 0
-        else:
-            src, dst, at = of(r.back, m), of(r.go, m), 1
-        return remote(src, dst, r.edge.at[at, 0, m], r.edge.at[at, 1, m], dict(section=1 - sec))
+        rows[0:NS, s] = -jnp.exp(rows[0:NS, s]) * LOG2E
 
     def forward(k, carry):
         m = k - sec
@@ -611,37 +654,31 @@
             def _():
                 boundary(RIGHT, m).wait_recv()
 
+            @pl.when(sec == 0)
+            def _():
+                load(m, 0).wait()
+
+            def gathering(hops):
+                if inside:
+
+                    @pl.when((sec == 0) & (m == 0))
+                    def _():
+                        rest(hops)
+
             u = of(r.u, m)
-            reset = r.reset[m]
+            reset = r.reset[m][:, 0:1]
             v = u[...].astype(f32)
             inv = lax.rsqrt(jnp.mean(v * v, axis=-1, keepdims=True) + EPS)
-            of(r.normed, m)[...] = (v * inv * gain[...]).astype(bf16)
-            f_x(reset, of(r.normed, m), win, rows, of(r.x, m), of(r.act, m))
+            normed, act, ssm = of(r.normed, m), of(r.act, m), of(r.ssm, m)
+            normed[...] = (v * inv * gain[...]).astype(bf16)
+            f_x(reset, normed, win, rows, of(r.x, m), act)
+            gathering((links.zs - 1,))
             f_rate(
-                reset,
-                of(r.act, m),
-                small,
-                rows,
-                of(r.proj, m),
-                of(r.rin, m),
-                of(r.pre, m),
-                r.dec,
-                r.gs,
-                r.cols,
-                r.diag,
+                reset, act, small, rows, of(r.proj, m), of(r.rin, m), of(r.pre, m), r.dec, r.gs, r.cols, r.diag
             )
-            f_scan(
-                of(r.act, m), rows, r.dec, r.gs, r.cols, r.diag, r.h.at[m], of(r.ssm, m)
-            )
-            if inside:
-
-                @pl.when((sec == 0) & (m == 0))
-                def _():
-                    gather.pump((2, 3), FORWARD)
-
-            f_out(
-                u, of(r.normed, m), win, wout, of(r.ssm, m), of(r.z, m), of(r.gated, m), r.section_out.at[m]
-            )
+            f_scan(act, rows, r.dec, r.gs, r.cols, r.diag, r.h.at[m], ssm)
+            gathering((links.zs,))
+            f_out(u, normed, win, wout, ssm, of(r.z, m), of(r.gated, m), r.section_out.at[m])
 
             @pl.when(sec == 0)
             def _():
@@ -650,8 +687,33 @@
         return carry
 
     lax.fori_loop(0, MICRO + 1, forward, 0)
-    if inside:
-        gather.pump((0, 1, 2, 3), FINISH)
+
+    @pl.when(sec == 1)
+    def _():
+        for m in range(MICRO):
+            load(m, 1).wait()
+
+    def products_out():
+        for c in range(DI // C):
+            s = pl.ds(c * C, C)
+            r.gwo[s, :] = tn(r.gated[:, s], r.go[...]).astype(r.gwo.dtype)
+
+    def products_in(lo):
+        for c in range(DI // C):
+            s = pl.ds(lo + c * C, C)
+            r.gwi[s, :] = tn(r.gm[:, s], r.normed[...]).astype(r.gwi.dtype)
+
+    def products_small():
+        for c in range(DI // C):
+            s = pl.ds(c * C, C)
+            r.gws[s, :] = (tn(r.act[:, s], r.gp[...]) + tn(r.gpre[:, s], r.rin[...])).astype(r.gws.dtype)
+        if inside:
+            sm, gg = r.sm[0:32, :], r.gg[...]
+            for i in range(n):
+                top = pltpu.roll(sm, -i * r2 % DI, 1)[:, 0:128]
+                g = pltpu.roll(gg, -i * gw % D, 1)[:, 0:128]
+                top = jnp.where(iota((32, 128), 0) == 23, jnp.broadcast_to(g, (32, 128)), top)
+                r.gwt[pl.ds(32 * i, 32), :] = top.astype(bf16)
 
     def backward(k, carry):
         m = k - (1 - sec)
@@ -663,30 +725,38 @@
                 boundary(LEFT, m).wait_recv()
 
             first = m == 0
-            reset = r.reset[m]
+            reset = r.reset[m][:, 0:1]
             go, gm, sm = of(r.go, m), of(r.gm, m), r.sm
             act, pre = of(r.act, m), of(r.pre, m)
             gs, gd, gr, gb, gc = r.gs, r.dec, r.gr, r.gb, r.gc
+
+            def last(*steps):
+                @pl.when(m == MICRO - 1)
+                def _():
+                    for step in steps:
+                        step()
+
+            def scattering(*steps):
+                if inside:
+                    last(*(functools.partial(stage, p) for stage, p in steps))
+
             b_gate(first, go, wout, of(r.z, m), of(r.ssm, m), act, gs, gm, sm)
+            last(products_out, lambda: products_in(DI))
+            if inside:
+                scattering((scatter.start, 0), (scatter.start, 1))
             b_prep(reset, pre, act, of(r.proj, m), r.dec, r.drive, r.cols, r.diag)
+            if inside:
+                scattering((scatter.across, 0))
             b_scan(
-                first,
-                gs,
-                rows,
-                r.dec,
-                r.cols,
-                r.diag,
-                r.drive,
-                r.h.at[m],
-                r.adj,
-                gd,
-                gr,
-                gb,
-                gc,
-                sm,
+                first, gs, rows, r.dec, r.cols, r.diag, r.drive, r.h.at[m], r.adj, gd, gr, gb, gc, sm
             )
+            if inside:
+                scattering((scatter.across, 1))
             b_pre(first, act, pre, small, gd, gr, gb, gc, of(r.gpre, m), of(r.gp, m), sm)
             b_conv(first, reset, rows, small, of(r.x, m), gs, gd, pre, of(r.gp, m), gm, sm)
+            last(lambda: products_in(0))
+            if inside:
+                scattering((scatter.start, 2))
             sg = r.section_grad.at[m]
             b_in(first, of(r.u, m), go, gain, win, gm, sg, r.gg)
 
@@ -698,41 +768,19 @@
         return carry
 
     lax.fori_loop(0, MICRO + 1, backward, 0)
-
-    gwi, gwo, gws = r.gwi, r.gwo, r.gws
-    for c in range(DI // C):
-        s = pl.ds(c * C, C)
-        gwo[s, :] = tn(r.gated[:, s], GO[...]).astype(gwo.dtype)
-    for c in range(2 * DI // C):
-        s = pl.ds(c * C, C)
-        gwi[s, :] = tn(r.gm[:, s], r.normed[...]).astype(gwi.dtype)
-    for c in range(DI // C):
-        s = pl.ds(c * C, C)
-        head = tn(r.act[:, s], r.gp[...]) + tn(r.gpre[:, s], r.rin[...])
-        gws[s, 0:128] = head.astype(gws.dtype)
-        tail = jnp.concatenate([r.sm[0:24, s], jnp.zeros((104, C), f32)], axis=0).T
-        gws[s, 128:256] = tail.astype(gws.dtype)
+    products_small()
     if inside:
-        lane = iota((16, 128), 1)
-        own = (iota((16, 128), 0) == 0) & (lane >= GAIN_LANE) & (lane < GAIN_LANE + gw)
-        for i in range(n):
-            moved = pltpu.roll(r.gg[...], (GAIN_LANE - i * gw) % D, 1)[:, 0:128]
-            at = pl.ds(i * r2, 16)
-            old = gws[at, 128:256].astype(f32)
-            gws[at, 128:256] = jnp.where(own, jnp.broadcast_to(moved, (16, 128)), old).astype(gws.dtype)
-        scatter = Scatter(
-            links,
-            [
-                (gwo, r.co, r.xo, r.uo, r.do, r.gout_shard, r2),
-                (gwi, r.ci, r.xi, r.ui, r.di, r.gin_shard, r1),
-                (gws, r.cs, r.xs, r.us, r.ds, r.gsmall_shard, r2),
-            ],
-            r.rs_core,
-            r.rs_line,
-        )
-        for stage in (scatter.start, scatter.across, scatter.line, scatter.finish):
-            for p in range(3):
-                stage(p)
+        for p in (3, 4):
+            scatter.start(p)
+        for p in (2, 3, 4):
+            scatter.across(p)
+        for p in range(5):
+            scatter.line(p)
+        for p in range(5):
+            scatter.own(p)
+        for p in range(5):
+            gather.finish(p)
+            scatter.finish(p)
 
     for m in range(MICRO):
 
@@ -753,6 +801,7 @@
         section_grad=((MICRO, T, D), f32),
     )
     scratch = dict(
+        reset=((MICRO, T, 128), f32),
         u=((rows2, D), bf16),
         go=((rows2, D), bf16),
         back=((rows2, D), bf16),
@@ -779,42 +828,66 @@
         cols=((T * NS, 128), f32),
         diag=((T, NS * TB), bf16),
         rows=((32, DI), f32),
-        sm=((32, DI), f32),
     )
-    sems = dict(edge=(2, 2, MICRO))
+    sems = dict(edge=(2, 2, MICRO), loads=(MICRO,))
     if inside:
-        outs |= dict(gin_shard=((r1, D), f32))
-        outs |= dict(gout_shard=((r2, D), f32))
-        outs |= dict(gsmall_shard=((r2, 256), f32))
-        scratch |= dict(gain=((1, D), f32))
-        scratch |= dict(gg=((1, D), f32))
-        scratch |= dict(win=((2 * DI, D), bf16))
-        scratch |= dict(wout=((DI, D), bf16))
-        scratch |= dict(small=((DI, 256), bf16))
-        scratch |= dict(gwi=((2 * DI, D), bf16))
-        scratch |= dict(gwo=((DI, D), bf16))
-        scratch |= dict(gws=((DI, 256), bf16))
-        two, one = 2 * zs, zs
-        scratch |= dict(ci=((two * r1, D), bf16), co=((two * r2, D), bf16), cs=((two * r2, 256), bf16))
-        scratch |= dict(xi=((one * r1, D), bf16), xo=((one * r2, D), bf16), xs=((one * r2, 256), bf16))
-        scratch |= dict(ui=((one * r1, D), bf16), uo=((one * r2, D), bf16), us=((one * r2, 256), bf16))
-        scratch |= dict(di=((one * r1, D), bf16), do=((one * r2, D), bf16), ds=((one * r2, 256), bf16))
-        sems |= dict(ag_line=(4, 3, zs))
-        sems |= dict(ag_core=(4, 2 * zs))
-        sems |= dict(ag_recv=(4, n))
-        sems |= dict(rs_core=(3, 2, 2 * zs))
-        sems |= dict(rs_line=(3, 6, zs))
+        outs |= dict(
+            gin_shard=((r1, D), f32),
+            gout_shard=((r2, D), f32),
+            gsmall_shard=((r2, 128), f32),
+            gtail_shard=((32, 128), f32),
+        )
+        scratch |= dict(
+            sm=((32, DI), f32),
+            gain=((1, D), f32),
+            gg=((1, D), f32),
+            win=((2 * DI, D), bf16),
+            wout=((DI, D), bf16),
+            small=((DI, 128), bf16),
+            tails=((32 * n, 128), bf16),
+            gwi=((2 * DI, D), bf16),
+            gwo=((DI, D), bf16),
+            gws=((DI, 128), bf16),
+            gwt=((32 * n, 128), bf16),
+            ci=((2 * zs * r1, D), bf16),
+            co=((2 * zs * r2, D), bf16),
+            cs=((2 * zs * r2, 128), bf16),
+            ct=((2 * zs * 32, 128), bf16),
+            xi=((zs * r1, D), bf16),
+            xo=((zs * r2, D), bf16),
+            xs=((zs * r2, 128), bf16),
+            xt=((zs * 32, 128), bf16),
+            ui=((zs * r1, D), bf16),
+            uo=((zs * r2, D), bf16),
+            us=((zs * r2, 128), bf16),
+            ut=((zs * 32, 128), bf16),
+            di=((zs * r1, D), bf16),
+            do=((zs * r2, D), bf16),
+            ds=((zs * r2, 128), bf16),
+            dt=((zs * 32, 128), bf16),
+        )
+        sems |= dict(
+            ag_line=(5, 3, zs),
+            ag_core=(5, 2 * zs),
+            ag_recv=(5, n),
+            rs_core=(5, 2, 2 * zs),
+            rs_line=(5, 6, zs),
+        )
     else:
-        outs |= dict(gwi=((2 * DI, D), f32))
-        outs |= dict(gwo=((DI, D), f32))
-        outs |= dict(gws=((DI, 256), f32))
-        outs |= dict(gg=((1, D), f32))
+        outs |= dict(
+            gwi=((2 * DI, D), f32),
+            gwo=((DI, D), f32),
+            gws=((DI, 128), f32),
+            gg=((1, D), f32),
+            sm=((32, DI), f32),
+        )
     names = list(arrays) + list(outs) + list(scratch) + list(sems)
     whole = pl.BlockSpec(memory_space=pltpu.VMEM)
+    far = pl.BlockSpec(memory_space=pl.ANY)
     results = pl.pallas_call(
         functools.partial(block, names, inside, n),
         out_shape=[jax.ShapeDtypeStruct(*spec) for spec in outs.values()],
-        in_specs=[whole] * len(arrays),
+        in_specs=[far] * 2 + [whole] * (len(arrays) - 2),
         out_specs=[whole] * len(outs),
         scratch_shapes=[pltpu.VMEM(*spec) for spec in scratch.values()]
         + [pltpu.SemaphoreType.DMA(shape) for shape in sems.values()],
@@ -826,75 +899,109 @@
     return types.SimpleNamespace(**dict(zip(outs, results)))
 
 
-def on_device(
-    inputs,
-    cotangent,
-    markers,
-    norm_gain,
-    in_proj,
-    conv_weight,
-    conv_bias,
-    x_proj,
-    dt_proj,
-    dt_bias,
-    a_log,
-    d_skip,
-    out_proj,
+def unpack(
+    out, grad, gin, gout, gsmall, gtail, out_o, grad_o, gain_o, in_o, cw_o, cb_o, x_o, dt_o, db_o, a_o, ds_o, po_o
 ):
+    r2, gw = cb_o.shape[1], gain_o.shape[1]
+    out_o[0] = out[...]
+    grad_o[0] = grad[...]
+    po_o[0] = gout[...]
+    in_o[...] = gin[...]
+    gain_o[...] = gtail[23:24, 0:gw]
+    cw_o[0] = gtail[NS : NS + KC, 0:r2]
+    cb_o[...] = gtail[20:21, 0:r2]
+    db_o[...] = gtail[21:22, 0:r2]
+    ds_o[...] = gtail[22:23, 0:r2]
+    a_o[...] = gtail[0:NS, 0:r2]
+    small = gsmall[...].T
+    x_o[...] = small[0 : RK + 2 * NS, :]
+    dt_o[0] = small[RK + 2 * NS : 128, :]
+
+
+def on_device(inputs, cotangent, markers, *weights):
+    (
+        norm_gain,
+        in_proj,
+        conv_weight,
+        conv_bias,
+        x_proj,
+        dt_proj,
+        dt_bias,
+        a_log,
+        d_skip,
+        out_proj,
+    ) = weights
     n = lax.axis_size(DP)
-    inside = n % 4 == 0 and (DI // n) % 16 == 0
-    r2, gw = DI // n, D // n
-    first = (jnp.arange(T) == 0)[None, :]
-    reset = jnp.where((markers > 0) | first, 1.0, 0.0).astype(f32)[:, :, None]
-    win = in_proj[0].T.astype(bf16)
-    wout = out_proj[0].astype(bf16)
-    gain = jnp.zeros((r2, 128 - GAIN_LANE), f32).at[0, 0:gw].set(norm_gain[0])
-    small = jnp.concatenate(
-        [
-            x_proj[0],
-            dt_proj[0].T,
-            a_log[0],
-            conv_weight[0].T,
-            conv_bias[0][:, None],
-            dt_bias[0][:, None],
-            d_skip[0][:, None],
-            jnp.zeros((r2, 1), f32),
-            gain,
-        ],
-        axis=1,
-    ).astype(bf16)
-    arrays = dict(inputs=inputs, cotangent=cotangent, reset=reset)
+    inside = n == 16
+    arrays = dict(inputs=inputs, cotangent=cotangent, markers=markers)
     if inside:
-        arrays |= dict(win_shard=win, wout_shard=wout, small_shard=small)
-        res = call(n, inside, arrays)
-        gin, gout, gsmall = res.gin_shard, res.gout_shard, res.gsmall_shard
-        ggain = gsmall[0, 128 + GAIN_LANE : 128 + GAIN_LANE + gw]
-    else:
-        gains = lax.all_gather(norm_gain.astype(bf16), DP, axis=1, tiled=True).astype(f32)
         arrays |= dict(
-            win=lax.all_gather(win, DP, axis=0, tiled=True),
-            wout=lax.all_gather(wout, DP, axis=0, tiled=True),
-            small=lax.all_gather(small, DP, axis=0, tiled=True),
-            gain=gains,
+            norm_gain=norm_gain,
+            in_proj=in_proj[0].T,
+            conv_weight=conv_weight,
+            conv_bias=conv_bias,
+            x_proj=x_proj[0].T,
+            dt_proj=dt_proj,
+            dt_bias=dt_bias,
+            a_log=a_log[0].T,
+            d_skip=d_skip,
+            out_proj=out_proj,
         )
         res = call(n, inside, arrays)
-        gin = lax.psum_scatter(res.gwi, DP, scatter_dimension=0, tiled=True)
-        gout = lax.psum_scatter(res.gwo, DP, scatter_dimension=0, tiled=True)
-        gsmall = lax.psum_scatter(res.gws, DP, scatter_dimension=0, tiled=True)
-        ggain = lax.psum_scatter(res.gg, DP, scatter_dimension=1, tiled=True)[0]
-    tail = gsmall[:, 128:]
+        whole = pl.BlockSpec(memory_space=pltpu.VMEM)
+        turned = (in_proj, x_proj, a_log)
+        shapes = [((1,) + res.section_out.shape, bf16), ((1,) + res.section_grad.shape, f32)]
+        shapes += [(w.shape[:0:-1] if any(w is t for t in turned) else w.shape, f32) for w in weights]
+        done = pl.pallas_call(
+            unpack,
+            out_shape=[jax.ShapeDtypeStruct(*spec) for spec in shapes],
+            in_specs=[whole] * 6,
+            out_specs=[whole] * 12,
+            name="unpack",
+        )(
+            res.section_out,
+            res.section_grad,
+            res.gin_shard,
+            res.gout_shard,
+            res.gsmall_shard,
+            res.gtail_shard,
+        )
+        grads = (g.T[None] if any(w is t for t in turned) else g for w, g in zip(weights, done[2:]))
+        return (*done[:2], *grads)
+
+    def gathered(value, axis):
+        return lax.all_gather(value.astype(bf16), DP, axis=axis, tiled=True)
+
+    r2 = DI // n
+    raw = jnp.concatenate(
+        [a_log[0].T, conv_weight[0], conv_bias, dt_bias, d_skip, jnp.zeros((9, r2), f32)], axis=0
+    )
+    arrays |= dict(
+        win=gathered(in_proj[0].T, 0),
+        wout=gathered(out_proj[0], 0),
+        small=gathered(jnp.concatenate([x_proj[0], dt_proj[0].T], axis=1), 0),
+        raw_rows=gathered(raw, 1).astype(f32),
+        gain=gathered(norm_gain, 1).astype(f32),
+    )
+    res = call(n, inside, arrays)
+
+    def scattered(value, axis):
+        return lax.psum_scatter(value, DP, scatter_dimension=axis, tiled=True)
+
+    gin, gout, gsmall = scattered(res.gwi, 0), scattered(res.gwo, 0), scattered(res.gws, 0)
+    rows = scattered(res.sm, 1)
     return (
         res.section_out[None],
         res.section_grad[None],
-        ggain[None],
+        scattered(res.gg, 1),
         gin.T[None],
-        tail[:, NS : NS + KC].T[None],
-        tail[:, 20][None],
+        rows[NS : NS + KC][None],
+        rows[20:21],
         gsmall[:, 0 : RK + 2 * NS][None],
         gsmall[:, RK + 2 * NS : 128].T[None],
-        tail[:, 21][None],
-        tail[:, 0:NS][None],
-        tail[:, 22][None],
+        rows[21:22],
+        rows[0:NS].T[None],
+        rows[22:23],
         gout[None],
     )
 

time: 224 us -> 193 us (0.86)
  Pallas kernels: 208 us -> 192 us
  local copies, waits for them, and re-layouts: 12.2 us -> 0 us
  other arithmetic: 2.56 us -> 0 us
    pallas_call x1, Pallas kernels: 208 us -> 189 us  [call(): pl.pallas_call(functools.partial(block, names, inside, n), out_shape=[jax...]
    unnamed x42 -> x0, local copies, waits for them, and re-layouts: 7.8 us -> none
    pallas_call x0 -> x1, Pallas kernels: none -> 2.91 us  [on_device(): pl.pallas_call(unpack, out_shape=[jax.ShapeDtypeStruct(*spec) for spec in...]
    convert_element_type x2 -> x0, other arithmetic: 2.53 us -> none  [the longest x1 1.86 us: on_device(): win = in_proj[0].T.astype(bf16)]
    slice x2 -> x0, local copies, waits for them, and re-layouts: 2.3 us -> none  [the longest x1 1.72 us: on_device(): tail[:, 22][None]]
where the time goes in v2:
time: 193 us; the launch traced here: 192 us
  Pallas kernels  192 us (99%)
    pallas_call x1, Pallas kernels, call(): pl.pallas_call(functools.partial(block, names, inside, n), out_shape=[jax...  189 us

profile of v2, /device:TPU:0, one launch (start us, length us, event | category | flops | bytes accessed | tf_op | source)
XLA Modules:
  0.0 192.4 jit_solution(10718480460415428512)
XLA Ops:
  0.6 188.8 %two_layer_block.1 = (bf16[2,128,768]{2,1,0:T(8,128)(2,1)}, f32[2,128,768]{2,1,0:T(8,128)}, f32[192,768]{1,0:T(8,128)}, f32[96,768]{1,0:T(8,128)}, f32[96,128]{1,0:T(8,128)}, /*index=5*/f32[32,128]{1,0:T(8,128)}) custom-call(bf16[2,128,768]{2,1,0:T(8,128)(2,1)} %refs_0_.1, bf16[2,128,768]{2,1,0:T(8,128)(2,1)} %refs_1_.1, s32[2,128]{1,0:T(2,128)} %refs_2_.1, ...), custom_call_target="tpu_custom_call" | custom-call | tf_op jit(solution)/shard_map/two_layer_block/pallas_call | solution.py:887
  189.4 2.9 %unpack.1 = (bf16[1,2,128,768]{3,2,1,0:T(8,128)(2,1)}, f32[1,2,128,768]{3,2,1,0:T(8,128)}, f32[1,48]{1,0:T(1,128)}, f32[192,768]{1,0:T(8,128)}, f32[1,4,96]{2,1,...) custom-call(bf16[2,128,768]{2,1,0:T(8,128)(2,1)} %get-tuple-element., ...), custom_call_target="tpu_custom_call" | custom-call | tf_op jit(solution)/shard_map/unpack/pallas_call | solution.py:955

commit v3 on v2

--- a/solution.py
+++ b/solution.py
@@ -52,10 +52,6 @@
     return 1.0 / (1.0 + jnp.exp(-v))
 
 
-def softplus(v):
-    return jnp.maximum(v, 0.0) + jnp.log1p(jnp.exp(-jnp.abs(v)))
-
-
 def wide(v):
     return jnp.concatenate([v] * (CS // 128), axis=1)
 
@@ -81,7 +77,7 @@
         dst[pl.ds(t * NS, NS), :] = jnp.broadcast_to(val[:, t : t + 1], (NS, 128))
 
 
-def f_x(reset, normed, win, rows, x_ref, act):
+def f_x(reset, normed, win, rows, x_ref, act, dact):
     keep = keeps(reset)
     for c in range(DI // C):
         s = pl.ds(c * C, C)
@@ -90,10 +86,12 @@
         v = rows[20:21, s] + rows[16:17, s] * x
         for k in range(1, KC):
             v = v + rows[16 + k : 17 + k, s] * (pltpu.roll(x, k, 0) * keep[k])
-        act[:, s] = (v * sigmoid(v)).astype(bf16)
-
-
-def f_rate(reset, act, small, rows, proj, rin, pre_ref, dec, drive, cols, diag):
+        sg = sigmoid(v)
+        act[:, s] = (v * sg).astype(bf16)
+        dact[:, s] = sg * (1.0 + v * (1.0 - sg))
+
+
+def f_rate(reset, act, small, rows, proj, rin, rate_ref, drate, dec, drive, drive_low, cols, diag):
     p = nn(act[...], small[:, 0:128])
     proj[...] = p
     lane_columns(cols, p.T[RK : RK + NS, :])
@@ -102,10 +100,14 @@
     for c in range(DI // C):
         s = pl.ds(c * C, C)
         pre = nt(rin[...], small[s, 0:128]) + rows[21:22, s]
-        pre_ref[:, s] = pre
-        rate = softplus(pre)
+        e = jnp.exp(-jnp.abs(pre))
+        rate = jnp.maximum(pre, 0.0) + jnp.log1p(e)
+        rate_ref[:, s] = rate
+        drate[:, s] = jnp.where(pre >= 0.0, 1.0, e) / (1.0 + e)
         dec[:, s] = jnp.where(reset > 0.0, BIG, rate)
-        drive[:, s] = rate * act[:, s].astype(f32)
+        both = rate * act[:, s].astype(f32)
+        drive[:, s] = both
+        drive_low[:, s] = both.astype(bf16)
 
 
 def f_scan(act, rows, dec, drive, cols, diag, h_ref, ssm):
@@ -137,13 +139,16 @@
     lax.fori_loop(0, NB // 4, sums, 0)
 
 
-def f_out(u, normed, win, wout, ssm, z_ref, gated, out):
+def f_out(u, normed, win, wout, ssm, sz_ref, dz_ref, gated, out):
     acc = u[...].astype(f32)
     for c in range(DI // C):
         s = pl.ds(c * C, C)
         z = nt(normed[...], win[pl.ds(DI + c * C, C), :])
-        z_ref[:, s] = z
-        g = (ssm[:, s] * (z * sigmoid(z))).astype(bf16)
+        sg = sigmoid(z)
+        sz = z * sg
+        sz_ref[:, s] = sz
+        dz_ref[:, s] = ssm[:, s] * (sg * (1.0 + z * (1.0 - sg)))
+        g = (ssm[:, s] * sz).astype(bf16)
         gated[:, s] = g
         acc = acc + nn(g, wout[s, :])
     out[...] = acc.astype(bf16)
@@ -153,32 +158,25 @@
     return jnp.where(first, value, old + value)
 
 
-def b_gate(first, go_ref, wout, z_ref, ssm, act, gs_ref, gm, sm):
+def b_gate(first, go_ref, wout, sz, dz, act, gs_ref, gm, sm):
     go = go_ref[...]
     for c in range(DI // C):
         s = pl.ds(c * C, C)
         gg = nt(go, wout[s, :])
-        z = z_ref[:, s]
-        sg = sigmoid(z)
-        gs = gg * z * sg
+        gs = gg * sz[:, s]
         gs_ref[:, s] = gs
-        gm[:, pl.ds(DI + c * C, C)] = (gg * ssm[:, s] * sg * (1.0 + z * (1.0 - sg))).astype(bf16)
+        gm[:, pl.ds(DI + c * C, C)] = (gg * dz[:, s]).astype(bf16)
         part = jnp.sum(gs * act[:, s].astype(f32), axis=0, keepdims=True)
         sm[22:23, s] = total(sm[22:23, s], first, part)
 
 
-def b_prep(reset, pre, act, proj, dec, drive, cols, diag):
+def b_prep(proj, cols, diag):
     p = proj[...]
     lane_columns(cols, p.T[RK + NS : RK + 2 * NS, :])
     diag[...] = block_diagonal(p[:, RK : RK + NS])
-    for c in range(DI // C):
-        s = pl.ds(c * C, C)
-        rate = softplus(pre[:, s])
-        dec[:, s] = jnp.where(reset > 0.0, BIG, rate)
-        drive[:, s] = (rate * act[:, s].astype(f32)).astype(bf16)
-
-
-def b_scan(first, gs, rows, dec, cols, diag, drive, h_ref, adj_ref, gd, gr, gb, gc, sm):
+
+
+def b_scan(between, first, gs, rows, dec, cols, diag, drive, h_ref, adj_ref, gd, gr, gb, gc, sm):
     ones = (iota((TB, TB * NS), 1) // NS) == iota((TB, TB * NS), 0)
     od = ones.astype(bf16)
 
@@ -227,13 +225,15 @@
             return carry
 
         lax.fori_loop(0, NB // 4, adjoint_sums, 0)
-
-
-def b_pre(first, act, pre, small, gd, gr, gb, gc, gpre, gp, sm):
+        if c == 0 and between is not None:
+            between()
+
+
+def b_pre(first, act, drate, small, gd, gr, gb, gc, gpre, gp, sm):
     acc = jnp.zeros((T, 128), f32)
     for c in range(DI // C):
         s = pl.ds(c * C, C)
-        g = ((gr[:, s] + gd[:, s] * act[:, s].astype(f32)) * sigmoid(pre[:, s])).astype(bf16)
+        g = ((gr[:, s] + gd[:, s] * act[:, s].astype(f32)) * drate[:, s]).astype(bf16)
         gpre[:, s] = g
         part = jnp.sum(g.astype(f32), axis=0, keepdims=True)
         sm[21:22, s] = total(sm[21:22, s], first, part)
@@ -246,26 +246,21 @@
     gp[...] = jnp.where(iota((T, 128), 1) < RK, pltpu.roll(acc, RK, 1), bc).astype(bf16)
 
 
-def b_conv(first, reset, rows, small, x_ref, gs, gd, pre, gp, gm, sm):
+def b_conv(first, reset, rows, small, x_ref, dact, gs, gd, rate, gp, gm, sm):
     keep = keeps(reset)
     for c in range(DI // C):
         s = pl.ds(c * C, C)
+        ga = gs[:, s] * rows[22:23, s] + gd[:, s] * rate[:, s] + nt(gp[...], small[s, 0:128])
+        gc = ga * dact[:, s]
         x = x_ref[:, s]
-        xs = [x] + [pltpu.roll(x, k, 0) * keep[k] for k in range(1, KC)]
-        v = rows[20:21, s]
-        for k in range(KC):
-            v = v + rows[16 + k : 17 + k, s] * xs[k]
-        ga = gs[:, s] * rows[22:23, s] + gd[:, s] * softplus(pre[:, s]) + nt(gp[...], small[s, 0:128])
-        sg = sigmoid(v)
-        gc = ga * sg * (1.0 + v * (1.0 - sg))
         part = jnp.sum(gc, axis=0, keepdims=True)
         sm[20:21, s] = total(sm[20:21, s], first, part)
-        gx = gc * rows[16:17, s]
+        gx = jnp.zeros((T, C), f32)
         for k in range(KC):
-            part = jnp.sum(gc * xs[k], axis=0, keepdims=True)
+            ahead = pltpu.roll(gc * keep[k], T - k, 0) if k else gc
+            part = jnp.sum(ahead * x, axis=0, keepdims=True)
             sm[16 + k : 17 + k, s] = total(sm[16 + k : 17 + k, s], first, part)
-            if k:
-                gx = gx + pltpu.roll(gc * keep[k], T - k, 0) * rows[16 + k : 17 + k, s]
+            gx = gx + ahead * rows[16 + k : 17 + k, s]
         gm[:, s] = gx.astype(bf16)
 
 
@@ -321,8 +316,8 @@
         pl.semaphore_wait(pltpu.get_barrier_semaphore(), 3 + ends)
 
 
-def part(ref, index, count):
-    return ref.at[pl.ds(pl.multiple_of(index * count, 16), count), :]
+def part(ref, index, count, first=0, rows=None):
+    return ref.at[pl.ds(pl.multiple_of(index * count + first, 16), rows or count), :]
 
 
 def remote(src, dst, send, recv, device):
@@ -420,7 +415,8 @@
                 self.each(p, side, r, crossed)
 
 
-def add_rows(dst, src, count):
+def add_rows(dst, src):
+    count = dst.shape[0]
     step = 48 if count % 48 == 0 else 16
 
     def add(i, carry):
@@ -436,17 +432,22 @@
         self.k, self.pieces = links, pieces
         self.core_sems, self.line_sems = core_sems, line_sems
 
-    def copy(self, p, route, z, x=None):
+    def rows(self, p, c, z, count=1):
+        g, first, _, _, _, _, size, _, _ = self.pieces[p]
+        return part(g, 1, first + (c * self.k.zs + z) * size, 0, count * size)
+
+    def mine(self, p, z):
+        return self.rows(p, self.k.c, z)
+
+    def copy(self, p, route, z=None):
         k = self.k
-        g, core, across, below, above, _, count, _, _ = self.pieces[p]
+        _, _, core, below, above, _, size, lo, hi = self.pieces[p]
         if route == CORE:
-            slot = 2 * z + x
-            send, recv = self.core_sems.at[p, 0, slot], self.core_sems.at[p, 1, slot]
-            src, dst = part(g, k.owner(z, x, 1 - k.c), count), part(core, slot, count)
+            send, recv = self.core_sems.at[p, 0], self.core_sems.at[p, 1]
+            src, dst = self.rows(p, 1 - k.c, lo, hi - lo), part(core, 1, lo * size, 0, (hi - lo) * size)
         else:
             send, recv = self.line_sems.at[p, 2 * route, z], self.line_sems.at[p, 2 * route + 1, z]
-            src = part(g, k.owner(z, 1 - k.x if route == ACROSS else k.x, k.c), count)
-            dst = part((below, above, across)[route], z, count)
+            src, dst = self.mine(p, z), part((below, above)[route], z, size)
         return remote(src, dst, send, recv, k.dev(route))
 
     def far_first(self, p):
@@ -460,33 +461,23 @@
             yield z
 
     def start(self, p):
-        for z in self.far_first(p):
-            for x in (1 - self.k.x, self.k.x):
-                self.copy(p, CORE, z, x).start()
-
-    def across(self, p):
-        k = self.k
-        g, core, count = self.pieces[p][0], self.pieces[p][1], self.pieces[p][6]
-        for z in self.far_first(p):
-            for x in (1 - k.x, k.x):
-                self.copy(p, CORE, z, x).wait_recv()
-                add_rows(part(g, k.owner(z, x, k.c), count), part(core, 2 * z + x, count), count)
-                if x is not k.x:
-                    self.copy(p, ACROSS, z).start()
+        self.copy(p, CORE).start()
+
+    def core(self, p):
+        _, _, core, _, _, _, size, lo, hi = self.pieces[p]
+        self.copy(p, CORE).wait_recv()
+        add_rows(self.rows(p, self.k.c, lo, hi - lo), part(core, 1, lo * size, 0, (hi - lo) * size))
 
     def line(self, p):
         k = self.k
-        g, _, across, below, above, _, count, _, _ = self.pieces[p]
+        _, _, _, below, above, _, size, _, _ = self.pieces[p]
         for z in self.far_first(p):
-            mine = part(g, k.owner(z, k.x, k.c), count)
-            self.copy(p, ACROSS, z).wait_recv()
-            add_rows(mine, part(across, z, count), count)
 
             def hop(route, inner, source):
                 @pl.when(inner)
                 def _():
                     self.copy(p, route, z).wait_recv()
-                    add_rows(mine, part(source, z, count), count)
+                    add_rows(self.mine(p, z), part(source, z, size))
 
                 self.copy(p, route, z).start()
 
@@ -500,28 +491,26 @@
 
     def own(self, p):
         k = self.k
-        g, _, _, below, above, result, count, lo, hi = self.pieces[p]
+        _, _, _, below, above, result, size, lo, hi = self.pieces[p]
 
         @pl.when((k.z >= lo) & (k.z < hi))
         def _():
-            result[...] = part(g, k.i, count)[...].astype(f32)
+            result[...] = self.mine(p, k.z)[...].astype(f32)
 
             @pl.when(k.z > 0)
             def _():
                 self.copy(p, UP, k.z).wait_recv()
-                add_rows(result, part(below, k.z, count), count)
+                add_rows(result, part(below, k.z, size))
 
             @pl.when(k.z < k.zs - 1)
             def _():
                 self.copy(p, DOWN, k.z).wait_recv()
-                add_rows(result, part(above, k.z, count), count)
+                add_rows(result, part(above, k.z, size))
 
     def finish(self, p):
         k = self.k
+        self.copy(p, CORE).wait_send()
         for z in range(*self.pieces[p][7:]):
-            for x in range(2):
-                self.copy(p, CORE, z, x).wait_send()
-            self.copy(p, ACROSS, z).wait_send()
 
             @pl.when(z > k.z)
             def _():
@@ -544,6 +533,7 @@
     sec = lax.axis_index(SECTION)
     links = Links(n)
     r1, r2, gw = 2 * DI // n, DI // n, D // n
+    r3 = r2 + 32
     rows, small, gain, win, wout = r.rows, r.small, r.gain, r.win, r.wout
 
     def of(ref, m):
@@ -622,18 +612,37 @@
             rest((links.zs - 1, links.zs))
 
         weight_rows(tails, rows, gain, n)
-        scatter = Scatter(
-            links,
-            [
-                (r.gwo, r.co, r.xo, r.uo, r.do, r.gout_shard, r2, 0, links.zs),
-                (r.gwi, r.ci, r.xi, r.ui, r.di, r.gin_shard, r1, half, links.zs),
-                (r.gwi, r.ci, r.xi, r.ui, r.di, r.gin_shard, r1, 0, half),
-                (r.gws, r.cs, r.xs, r.us, r.ds, r.gsmall_shard, r2, 0, links.zs),
-                (r.gwt, r.ct, r.xt, r.ut, r.dt, r.gtail_shard, 32, 0, links.zs),
-            ],
-            r.rs_core,
-            r.rs_line,
-        )
+        half_rows = 2 * links.zs
+        pieces = [
+            (r.gwo, 0, r.co, r.uo, r.do, r.gout_shard, r2, 0, links.zs),
+            (r.gwi, 0, r.ci, r.ui, r.di, r.gin_shard, r1, half, links.zs),
+            (r.gwi, 0, r.ci, r.ui, r.di, r.gin_shard, r1, 0, half),
+            (r.gws, links.x * half_rows * r3, r.cs, None, None, None, r3, 0, links.zs),
+        ]
+        scatter = Scatter(links, pieces, r.rs_core, r.rs_line)
+        strip = 2 * r1
+
+        def operand(kind, m, zz=0):
+            src = of((r.gated, r.normed, r.go, r.gm)[kind], m)
+            dst = of((r.xg, r.xn, r.xo, r.xm)[kind], m)
+            if kind == 3:
+                at = pl.multiple_of((2 * zz + 1 - links.x) * strip, 128)
+                src, dst = src.at[:, pl.ds(at, strip)], dst.at[:, pl.ds(zz * strip, strip)]
+            sems = r.xs_sems.at[kind + zz, m]
+            return remote(src, dst, sems.at[0], sems.at[1], links.dev(ACROSS))
+
+        def small_across():
+            sems = r.xs_sems.at[7, 0]
+            src = part(r.gws, 1 - links.x, half_rows * r3)
+            return remote(src, r.xs, sems.at[0], sems.at[1], links.dev(ACROSS))
+
+        def small_direct(act):
+            for step in range(1, links.zs):
+                to = (links.z + step) % links.zs
+                sems = r.xs_sems.at[7, step]
+                dst = part(r.ss, step, r3)
+                act(remote(scatter.mine(3, to), dst, sems.at[0], sems.at[1], dict(dp=links.owner(to, links.x, links.c))))
+
     else:
         sem = pltpu.get_barrier_semaphore()
         pl.semaphore_signal(
@@ -669,20 +678,36 @@
             reset = r.reset[m][:, 0:1]
             v = u[...].astype(f32)
             inv = lax.rsqrt(jnp.mean(v * v, axis=-1, keepdims=True) + EPS)
-            normed, act, ssm = of(r.normed, m), of(r.act, m), of(r.ssm, m)
+            normed, act, ssm = of(r.normed, m), of(r.act, m), r.gr
             normed[...] = (v * inv * gain[...]).astype(bf16)
-            f_x(reset, normed, win, rows, of(r.x, m), act)
+            f_x(reset, normed, win, rows, of(r.x, m), act, of(r.dact, m))
             gathering((links.zs - 1,))
             f_rate(
-                reset, act, small, rows, of(r.proj, m), of(r.rin, m), of(r.pre, m), r.dec, r.gs, r.cols, r.diag
+                reset,
+                act,
+                small,
+                rows,
+                of(r.proj, m),
+                of(r.rin, m),
+                of(r.rate, m),
+                of(r.drate, m),
+                of(r.dec, m),
+                r.gs,
+                of(r.drive, m),
+                r.cols,
+                r.diag,
             )
-            f_scan(act, rows, r.dec, r.gs, r.cols, r.diag, r.h.at[m], ssm)
+            f_scan(act, rows, of(r.dec, m), r.gs, r.cols, r.diag, r.h.at[m], ssm)
             gathering((links.zs,))
-            f_out(u, normed, win, wout, ssm, of(r.z, m), of(r.gated, m), r.section_out.at[m])
+            f_out(u, normed, win, wout, ssm, of(r.sz, m), of(r.dz, m), of(r.gated, m), r.section_out.at[m])
 
             @pl.when(sec == 0)
             def _():
                 boundary(RIGHT, m).start()
+
+            if inside:
+                operand(0, m).start()
+                operand(1, m).start()
 
         return carry
 
@@ -693,27 +718,86 @@
         for m in range(MICRO):
             load(m, 1).wait()
 
+    def owners_rows(g, first, size, zz, value):
+        for c in range(2):
+            at = pl.ds(pl.multiple_of(first + (c * links.zs + zz) * size, 16), size)
+            g[at, :] = value[c * size : (c + 1) * size].astype(g.dtype)
+
     def products_out():
+        if inside:
+            for kind in (0, 2):
+                for m in range(MICRO):
+                    operand(kind, m).wait_recv()
+            for zz in range(links.zs):
+                s = pl.ds(zz * 4 * r2, 4 * r2)
+                full = tn(r.gated[:, s], r.go[...]) + tn(r.xg[:, s], r.xo[...])
+                owners_rows(r.gwo, 0, r2, zz, jnp.where(links.x == 0, full[: 2 * r2], full[2 * r2 :]))
+        else:
+            for c in range(DI // C):
+                s = pl.ds(c * C, C)
+                r.gwo[s, :] = tn(r.gated[:, s], r.go[...])
+
+    def products_in(zzs):
+        if inside:
+            for m in range(MICRO):
+                if half in zzs:
+                    operand(1, m).wait_recv()
+                for zz in zzs:
+                    operand(3, m, zz).wait_recv()
+            for zz in zzs:
+                mine = pl.ds(pl.multiple_of((2 * zz + links.x) * strip, 128), strip)
+                full = tn(r.gm[:, mine], r.normed[...]) + tn(r.xm[:, pl.ds(zz * strip, strip)], r.xn[...])
+                owners_rows(r.gwi, 0, r1, zz, full)
+        else:
+            for c in range(2 * DI // C):
+                s = pl.ds(c * C, C)
+                r.gwi[s, :] = tn(r.gm[:, s], r.normed[...])
+
+    def products_head():
         for c in range(DI // C):
             s = pl.ds(c * C, C)
-            r.gwo[s, :] = tn(r.gated[:, s], r.go[...]).astype(r.gwo.dtype)
-
-    def products_in(lo):
-        for c in range(DI // C):
-            s = pl.ds(lo + c * C, C)
-            r.gwi[s, :] = tn(r.gm[:, s], r.normed[...]).astype(r.gwi.dtype)
+            value = tn(r.act[:, s], r.gp[...]) + tn(r.gpre[:, s], r.rin[...])
+            if inside:
+                r.head[s, :] = value
+            else:
+                r.gws[s, :] = value
 
     def products_small():
-        for c in range(DI // C):
-            s = pl.ds(c * C, C)
-            r.gws[s, :] = (tn(r.act[:, s], r.gp[...]) + tn(r.gpre[:, s], r.rin[...])).astype(r.gws.dtype)
-        if inside:
-            sm, gg = r.sm[0:32, :], r.gg[...]
-            for i in range(n):
-                top = pltpu.roll(sm, -i * r2 % DI, 1)[:, 0:128]
-                g = pltpu.roll(gg, -i * gw % D, 1)[:, 0:128]
-                top = jnp.where(iota((32, 128), 0) == 23, jnp.broadcast_to(g, (32, 128)), top)
-                r.gwt[pl.ds(32 * i, 32), :] = top.astype(bf16)
+        sm, gg = r.sm[0:32, :], r.gg[...]
+        for i in range(n):
+            z, x, c = i // 4, (i // 2) % 2, i % 2
+            to = ((x * 2 + c) * links.zs + z) * r3
+            r.gws[pl.ds(to, r2), :] = r.head[pl.ds(i * r2, r2), :].astype(bf16)
+            top = pltpu.roll(sm, -i * r2 % DI, 1)[:, 0:128]
+            g = pltpu.roll(gg, -i * gw % D, 1)[:, 0:128]
+            top = jnp.where(iota((32, 128), 0) == 23, jnp.broadcast_to(g, (32, 128)), top)
+            r.gws[pl.ds(to + r2, 32), :] = top.astype(bf16)
+
+    if inside:
+        low, high = range(half), range(half, links.zs)
+        end = (links.z == 0) | (links.z == links.zs - 1)
+
+        def first_products():
+            products_out()
+            scatter.start(0)
+
+        def second_products():
+            scatter.core(0)
+            products_in(high)
+            scatter.start(1)
+
+            @pl.when(end)
+            def _():
+                scatter.line(0)
+
+        def fourth_step():
+            products_small()
+            small_across().start()
+            scatter.core(1)
+
+            @pl.when(end)
+            def _():
+                scatter.line(1)
 
     def backward(k, carry):
         m = k - (1 - sec)
@@ -727,36 +811,33 @@
             first = m == 0
             reset = r.reset[m][:, 0:1]
             go, gm, sm = of(r.go, m), of(r.gm, m), r.sm
-            act, pre = of(r.act, m), of(r.pre, m)
-            gs, gd, gr, gb, gc = r.gs, r.dec, r.gr, r.gb, r.gc
-
-            def last(*steps):
-                @pl.when(m == MICRO - 1)
+            act, dec = of(r.act, m), of(r.dec, m)
+            gs, gd, gr, gb, gc = r.gs, dec, r.gr, r.gb, r.gc
+
+            def early(step):
+                @pl.when((m == MICRO - 1) & (sec == 0))
                 def _():
-                    for step in steps:
-                        step()
-
-            def scattering(*steps):
-                if inside:
-                    last(*(functools.partial(stage, p) for stage, p in steps))
-
-            b_gate(first, go, wout, of(r.z, m), of(r.ssm, m), act, gs, gm, sm)
-            last(products_out, lambda: products_in(DI))
+                    step()
+
             if inside:
-                scattering((scatter.start, 0), (scatter.start, 1))
-            b_prep(reset, pre, act, of(r.proj, m), r.dec, r.drive, r.cols, r.diag)
+                operand(2, m).start()
+            b_gate(first, go, wout, of(r.sz, m), of(r.dz, m), act, gs, gm, sm)
             if inside:
-                scattering((scatter.across, 0))
+                for zz in high:
+                    operand(3, m, zz).start()
+            b_prep(of(r.proj, m), r.cols, r.diag)
             b_scan(
-                first, gs, rows, r.dec, r.cols, r.diag, r.drive, r.h.at[m], r.adj, gd, gr, gb, gc, sm
+                (lambda: early(first_products)) if inside else None,
+                first, gs, rows, dec, r.cols, r.diag, of(r.drive, m), r.h.at[m], r.adj, gd, gr, gb, gc, sm
             )
             if inside:
-                scattering((scatter.across, 1))
-            b_pre(first, act, pre, small, gd, gr, gb, gc, of(r.gpre, m), of(r.gp, m), sm)
-            b_conv(first, reset, rows, small, of(r.x, m), gs, gd, pre, of(r.gp, m), gm, sm)
-            last(lambda: products_in(0))
+                early(second_products)
+            b_pre(first, act, of(r.drate, m), small, gd, gr, gb, gc, of(r.gpre, m), of(r.gp, m), sm)
+            b_conv(first, reset, rows, small, of(r.x, m), of(r.dact, m), gs, gd, of(r.rate, m), of(r.gp, m), gm, sm)
             if inside:
-                scattering((scatter.start, 2))
+                for zz in low:
+                    operand(3, m, zz).start()
+                early(products_head)
             sg = r.section_grad.at[m]
             b_in(first, of(r.u, m), go, gain, win, gm, sg, r.gg)
 
@@ -765,22 +846,71 @@
                 of(r.back, m)[...] = sg[...].astype(bf16)
                 boundary(LEFT, m).start()
 
+            if inside:
+                early(fourth_step)
+
         return carry
 
     lax.fori_loop(0, MICRO + 1, backward, 0)
-    products_small()
     if inside:
-        for p in (3, 4):
-            scatter.start(p)
-        for p in (2, 3, 4):
-            scatter.across(p)
-        for p in range(5):
-            scatter.line(p)
-        for p in range(5):
+
+        @pl.when(sec == 1)
+        def _():
+            first_products()
+            second_products()
+            products_head()
+            fourth_step()
+
+        @pl.when(jnp.logical_not(end))
+        def _():
+            scatter.line(0)
+
+        products_in(low)
+        scatter.start(2)
+        small_across().wait_recv()
+        add_rows(part(r.gws, links.x, half_rows * r3), r.xs)
+        scatter.start(3)
+
+        @pl.when(jnp.logical_not(end))
+        def _():
+            scatter.line(1)
+
+        scatter.core(2)
+
+        @pl.when(end)
+        def _():
+            scatter.line(2)
+
+        scatter.core(3)
+        small_direct(lambda copy: copy.start())
+
+        @pl.when(jnp.logical_not(end))
+        def _():
+            scatter.line(2)
+
+        small_direct(lambda copy: copy.wait_recv())
+        total_small = scatter.mine(3, links.z)[...].astype(f32)
+        for step in range(1, links.zs):
+            total_small = total_small + part(r.ss, step, r3)[...].astype(f32)
+        r.gsmall_shard[...] = total_small
+        for p in range(3):
             scatter.own(p)
-        for p in range(5):
+        for p in range(3):
+            scatter.finish(p)
+        scatter.copy(3, CORE).wait_send()
+        small_direct(lambda copy: copy.wait_send())
+        for p in range(len(gather.pieces)):
             gather.finish(p)
-            scatter.finish(p)
+        for m in range(MICRO):
+            for kind in range(3):
+                operand(kind, m).wait_send()
+            for zz in range(links.zs):
+                operand(3, m, zz).wait_send()
+        small_across().wait_send()
+    else:
+        products_out()
+        products_in(None)
+        products_head()
 
     for m in range(MICRO):
 
@@ -807,9 +937,11 @@
         back=((rows2, D), bf16),
         normed=((rows2, D), bf16),
         x=((rows2, DI), f32),
-        z=((rows2, DI), f32),
-        pre=((rows2, DI), f32),
-        ssm=((rows2, DI), f32),
+        dact=((rows2, DI), f32),
+        sz=((rows2, DI), f32),
+        dz=((rows2, DI), f32),
+        rate=((rows2, DI), f32),
+        drate=((rows2, DI), f32),
         act=((rows2, DI), bf16),
         gated=((rows2, DI), bf16),
         gpre=((rows2, DI), bf16),
@@ -819,12 +951,12 @@
         gp=((rows2, 128), bf16),
         h=((MICRO, (T + 1) * NS, DI), bf16),
         adj=((T * NS, CS), bf16),
-        dec=((T, DI), f32),
+        dec=((rows2, DI), f32),
         gs=((T, DI), f32),
         gr=((T, DI), f32),
         gb=((T, NS * TB), f32),
         gc=((T, NS * TB), bf16),
-        drive=((T, DI), bf16),
+        drive=((rows2, DI), bf16),
         cols=((T * NS, 128), f32),
         diag=((T, NS * TB), bf16),
         rows=((32, DI), f32),
@@ -834,8 +966,7 @@
         outs |= dict(
             gin_shard=((r1, D), f32),
             gout_shard=((r2, D), f32),
-            gsmall_shard=((r2, 128), f32),
-            gtail_shard=((32, 128), f32),
+            gsmall_shard=((r2 + 32, 128), f32),
         )
         scratch |= dict(
             sm=((32, DI), f32),
@@ -845,33 +976,31 @@
             wout=((DI, D), bf16),
             small=((DI, 128), bf16),
             tails=((32 * n, 128), bf16),
-            gwi=((2 * DI, D), bf16),
-            gwo=((DI, D), bf16),
-            gws=((DI, 128), bf16),
-            gwt=((32 * n, 128), bf16),
-            ci=((2 * zs * r1, D), bf16),
-            co=((2 * zs * r2, D), bf16),
-            cs=((2 * zs * r2, 128), bf16),
-            ct=((2 * zs * 32, 128), bf16),
-            xi=((zs * r1, D), bf16),
-            xo=((zs * r2, D), bf16),
-            xs=((zs * r2, 128), bf16),
-            xt=((zs * 32, 128), bf16),
+            gwi=((DI, D), bf16),
+            gwo=((DI // 2, D), bf16),
+            gws=((n * (r2 + 32), 128), bf16),
+            head=((DI, 128), f32),
+            xg=((rows2, DI), bf16),
+            xn=((rows2, D), bf16),
+            xo=((rows2, D), bf16),
+            xm=((rows2, DI), bf16),
+            ci=((zs * r1, D), bf16),
+            co=((zs * r2, D), bf16),
+            cs=((zs * (r2 + 32), 128), bf16),
+            xs=((2 * zs * (r2 + 32), 128), bf16),
+            ss=((zs * (r2 + 32), 128), bf16),
             ui=((zs * r1, D), bf16),
             uo=((zs * r2, D), bf16),
-            us=((zs * r2, 128), bf16),
-            ut=((zs * 32, 128), bf16),
             di=((zs * r1, D), bf16),
             do=((zs * r2, D), bf16),
-            ds=((zs * r2, 128), bf16),
-            dt=((zs * 32, 128), bf16),
         )
         sems |= dict(
             ag_line=(5, 3, zs),
             ag_core=(5, 2 * zs),
             ag_recv=(5, n),
-            rs_core=(5, 2, 2 * zs),
-            rs_line=(5, 6, zs),
+            rs_core=(4, 2),
+            rs_line=(3, 4, zs),
+            xs_sems=(8, max(MICRO, zs), 2),
         )
     else:
         outs |= dict(
@@ -900,20 +1029,21 @@
 
 
 def unpack(
-    out, grad, gin, gout, gsmall, gtail, out_o, grad_o, gain_o, in_o, cw_o, cb_o, x_o, dt_o, db_o, a_o, ds_o, po_o
+    out, grad, gin, gout, gsmall, out_o, grad_o, gain_o, in_o, cw_o, cb_o, x_o, dt_o, db_o, a_o, ds_o, po_o
 ):
     r2, gw = cb_o.shape[1], gain_o.shape[1]
     out_o[0] = out[...]
     grad_o[0] = grad[...]
     po_o[0] = gout[...]
     in_o[...] = gin[...]
-    gain_o[...] = gtail[23:24, 0:gw]
-    cw_o[0] = gtail[NS : NS + KC, 0:r2]
-    cb_o[...] = gtail[20:21, 0:r2]
-    db_o[...] = gtail[21:22, 0:r2]
-    ds_o[...] = gtail[22:23, 0:r2]
-    a_o[...] = gtail[0:NS, 0:r2]
-    small = gsmall[...].T
+    tail = gsmall[pl.ds(r2, 32), :]
+    gain_o[...] = tail[23:24, 0:gw]
+    cw_o[0] = tail[NS : NS + KC, 0:r2]
+    cb_o[...] = tail[20:21, 0:r2]
+    db_o[...] = tail[21:22, 0:r2]
+    ds_o[...] = tail[22:23, 0:r2]
+    a_o[...] = tail[0:NS, 0:r2]
+    small = gsmall[pl.ds(0, r2), :].T
     x_o[...] = small[0 : RK + 2 * NS, :]
     dt_o[0] = small[RK + 2 * NS : 128, :]
 
@@ -955,7 +1085,7 @@
         done = pl.pallas_call(
             unpack,
             out_shape=[jax.ShapeDtypeStruct(*spec) for spec in shapes],
-            in_specs=[whole] * 6,
+            in_specs=[whole] * 5,
             out_specs=[whole] * 12,
             name="unpack",
         )(
@@ -964,7 +1094,6 @@
             res.gin_shard,
             res.gout_shard,
             res.gsmall_shard,
-            res.gtail_shard,
         )
         grads = (g.T[None] if any(w is t for t in turned) else g for w, g in zip(weights, done[2:]))
         return (*done[:2], *grads)

time: 193 us -> 177 us (0.917)
  Pallas kernels: 192 us -> 176 us
    pallas_call x1, Pallas kernels: 189 us -> 174 us  [call(): pl.pallas_call(functools.partial(block, names, inside, n), out_shape=[jax...]
where the time goes in v3:
time: 177 us
  Pallas kernels  176 us (99%)
    pallas_call x1, Pallas kernels, call(): pl.pallas_call(functools.partial(block, names, inside, n), out_shape=[jax...  174 us

profile of v3, /device:TPU:0, one launch (start us, length us, event | category | flops | bytes accessed | tf_op | source)
XLA Modules:
  0.0 177.2 jit_solution(15755723487774721539)
XLA Ops:
  0.6 173.5 %two_layer_block.1 = (bf16[2,128,768]{2,1,0:T(8,128)(2,1)}, f32[2,128,768]{2,1,0:T(8,128)}, f32[192,768]{1,0:T(8,128)}, f32[96,768]{1,0:T(8,128)}, f32[128,128]{1,0:T(8,128)}) custom-call(bf16[2,128,768]{2,1,0:T(8,128)(2,1)} %refs_0_.1, bf16[2,128,768]{2,1,0:T(8,128)(2,1)} %refs_1_.1, s32[2,128]{1,0:T(2,128)} %refs_2_.1, f32[1,48]{1,0:T(1,128)} %refs_3_.1, ...), custom_call_target="tpu_custom_call" | custom-call | tf_op jit(solution)/shard_map/two_layer_block/pallas_call | solution.py:1016
  174.2 2.9 %unpack.1 = (bf16[1,2,128,768]{3,2,1,0:T(8,128)(2,1)}, f32[1,2,128,768]{3,2,1,0:T(8,128)}, f32[1,48]{1,0:T(1,128)}, f32[192,768]{1,0:T(8,128)}, f32[1,4,96]{2,1,...) custom-call(bf16[2,128,768]{2,1,0:T(8,128)(2,1)} %get-tuple-element., ...), custom_call_target="tpu_custom_call" | custom-call | tf_op jit(solution)/shard_map/unpack/pallas_call | solution.py:1085

commit v4 on v3

--- a/solution.py
+++ b/solution.py
@@ -332,17 +332,17 @@
 
 
 class Gather:
-    def __init__(self, links, pieces, line_send, core_send, recv):
-        self.k, self.pieces = links, pieces
+    def __init__(self, links, pieces, balanced, line_send, core_send, recv):
+        self.k, self.pieces, self.balanced = links, pieces, balanced
         self.line_send, self.core_send, self.recv = line_send, core_send, recv
 
-    def copy(self, p, z, x, c, route):
+    def copy(self, p, z, x, c, route, slot=None):
         whole, count = self.pieces[p][:2]
         ref = part(whole, self.k.owner(z, x, c), count)
         if route == CORE:
             send = self.core_send.at[p, 2 * z + x]
         else:
-            send = self.line_send.at[p, route, z]
+            send = self.line_send.at[p, route if slot is None else slot, z]
         return remote(ref, ref, send, self.recv.at[p, self.k.owner(z, x, c)], self.k.dev(route))
 
     def each(self, p, side, r, act):
@@ -370,7 +370,10 @@
             copy = self.copy(p, z, k.x, k.c, route)
             copy.wait_send() if do == FINISH else copy.start()
 
-        one(ACROSS)
+        @pl.when(jnp.logical_not(self.by_line(p, z)))
+        def _():
+            one(ACROSS)
+
         if side != ABOVE:
 
             @pl.when(k.z < k.zs - 1)
@@ -384,6 +387,31 @@
                 one(DOWN)
 
         one(CORE)
+
+    def by_line(self, p, z):
+        k = self.k
+        last = k.zs - 1
+        near = ((k.z == 1) & (z == 0)) | ((k.z == last - 1) & (z == last))
+        if p not in self.balanced:
+            return near
+        return near | ((k.z == 0) & (z == last)) | ((k.z == last) & (z == 0))
+
+    def relay(self, p, z, do):
+        k = self.k
+        last = k.zs - 1
+        far = int(p in self.balanced)
+
+        def one(route):
+            copy = self.copy(p, z, 1 - k.x, k.c, route, 3)
+            copy.wait_send() if do == FINISH else copy.start()
+
+        @pl.when(((k.z == 0) & (z == 0)) | ((k.z == last - 1) & (z == 0) & (far == 1)))
+        def _():
+            one(UP)
+
+        @pl.when(((k.z == last) & (z == last)) | ((k.z == 1) & (z == last) & (far == 1)))
+        def _():
+            one(DOWN)
 
     def start(self, p):
         self.each(p, BELOW, 0, lambda z: self.go(p, z, None, START))
@@ -392,6 +420,7 @@
         def pass_on(z):
             copy = self.copy(p, z, 1 - self.k.x, self.k.c, CORE)
             copy.wait_recv()
+            self.relay(p, z, START)
             copy.start()
 
         self.each(p, BELOW, r, pass_on)
@@ -408,6 +437,7 @@
 
         def crossed(z):
             self.copy(p, z, 1 - k.x, k.c, CORE).wait_send()
+            self.relay(p, z, FINISH)
 
         for r in range(k.zs):
             for side in (BELOW, ABOVE) if r else (BELOW,):
@@ -428,26 +458,32 @@
 
 
 class Scatter:
-    def __init__(self, links, pieces, core_sems, line_sems):
-        self.k, self.pieces = links, pieces
+    def __init__(self, links, pieces, subs, core_sems, line_sems):
+        self.k, self.pieces, self.subs = links, pieces, subs
         self.core_sems, self.line_sems = core_sems, line_sems
 
     def rows(self, p, c, z, count=1):
         g, first, _, _, _, _, size, _, _ = self.pieces[p]
         return part(g, 1, first + (c * self.k.zs + z) * size, 0, count * size)
 
-    def mine(self, p, z):
-        return self.rows(p, self.k.c, z)
-
-    def copy(self, p, route, z=None):
+    def mine(self, p, z, sub=None):
+        whole = self.rows(p, self.k.c, z)
+        return whole if sub is None else self.half(p, whole, sub)
+
+    def half(self, p, ref, sub):
+        count = ref.shape[0] // self.subs[p]
+        return ref.at[pl.ds(sub * count, count), :]
+
+    def copy(self, p, route, z=None, sub=0):
         k = self.k
         _, _, core, below, above, _, size, lo, hi = self.pieces[p]
         if route == CORE:
             send, recv = self.core_sems.at[p, 0], self.core_sems.at[p, 1]
             src, dst = self.rows(p, 1 - k.c, lo, hi - lo), part(core, 1, lo * size, 0, (hi - lo) * size)
         else:
-            send, recv = self.line_sems.at[p, 2 * route, z], self.line_sems.at[p, 2 * route + 1, z]
-            src, dst = self.mine(p, z), part((below, above)[route], z, size)
+            at = 4 * sub + 2 * route
+            send, recv = self.line_sems.at[p, at, z], self.line_sems.at[p, at + 1, z]
+            src, dst = self.mine(p, z, sub), self.half(p, part((below, above)[route], z, size), sub)
         return remote(src, dst, send, recv, k.dev(route))
 
     def far_first(self, p):
@@ -474,12 +510,14 @@
         for z in self.far_first(p):
 
             def hop(route, inner, source):
-                @pl.when(inner)
-                def _():
-                    self.copy(p, route, z).wait_recv()
-                    add_rows(self.mine(p, z), part(source, z, size))
-
-                self.copy(p, route, z).start()
+                for sub in range(self.subs[p]):
+
+                    @pl.when(inner)
+                    def _():
+                        self.copy(p, route, z, sub).wait_recv()
+                        add_rows(self.mine(p, z, sub), self.half(p, part(source, z, size), sub))
+
+                    self.copy(p, route, z, sub).start()
 
             @pl.when(z > k.z)
             def _():
@@ -496,29 +534,33 @@
         @pl.when((k.z >= lo) & (k.z < hi))
         def _():
             result[...] = self.mine(p, k.z)[...].astype(f32)
-
-            @pl.when(k.z > 0)
-            def _():
-                self.copy(p, UP, k.z).wait_recv()
-                add_rows(result, part(below, k.z, size))
-
-            @pl.when(k.z < k.zs - 1)
-            def _():
-                self.copy(p, DOWN, k.z).wait_recv()
-                add_rows(result, part(above, k.z, size))
+            for sub in range(self.subs[p]):
+
+                def take(route, source):
+                    self.copy(p, route, k.z, sub).wait_recv()
+                    add_rows(self.half(p, result, sub), self.half(p, part(source, k.z, size), sub))
+
+                @pl.when(k.z > 0)
+                def _():
+                    take(UP, below)
+
+                @pl.when(k.z < k.zs - 1)
+                def _():
+                    take(DOWN, above)
 
     def finish(self, p):
         k = self.k
         self.copy(p, CORE).wait_send()
         for z in range(*self.pieces[p][7:]):
-
-            @pl.when(z > k.z)
-            def _():
-                self.copy(p, UP, z).wait_send()
-
-            @pl.when(z < k.z)
-            def _():
-                self.copy(p, DOWN, z).wait_send()
+            for sub in range(self.subs[p]):
+
+                @pl.when(z > k.z)
+                def _():
+                    self.copy(p, UP, z, sub).wait_send()
+
+                @pl.when(z < k.z)
+                def _():
+                    self.copy(p, DOWN, z, sub).wait_send()
 
 
 def weight_rows(tails, rows, gain, n):
@@ -534,6 +576,14 @@
     links = Links(n)
     r1, r2, gw = 2 * DI // n, DI // n, D // n
     r3 = r2 + 32
+    if inside:
+        far_in = (r.markers, r.norm_gain, r.in_proj, r.conv_weight, r.conv_bias, r.x_proj)
+        far_in += (r.dt_proj, r.dt_bias, r.a_log, r.d_skip, r.out_proj)
+        near_in = (r.v_markers, r.v_norm_gain, r.v_in_proj, r.v_conv_weight, r.v_conv_bias, r.v_x_proj)
+        near_in += (r.v_dt_proj, r.v_dt_bias, r.v_a_log, r.v_d_skip, r.v_out_proj)
+    else:
+        far_in = (r.markers, r.all_win, r.all_wout, r.all_small, r.raw_rows, r.all_gain)
+        near_in = (r.v_markers, r.win, r.wout, r.small, r.v_raw_rows, r.gain)
     rows, small, gain, win, wout = r.rows, r.small, r.gain, r.win, r.wout
 
     def of(ref, m):
@@ -543,34 +593,47 @@
         src, dst = ((r.inputs, r.u), (r.cotangent, r.go))[at]
         return pltpu.make_async_copy(src.at[m], of(dst, m), r.loads.at[m])
 
+    if inside:
+        links.greet()
+    fetches = [
+        pltpu.make_async_copy(src, dst, r.fetch.at[at])
+        for at, (src, dst) in enumerate(zip(far_in, near_in, strict=True))
+    ]
+    for fetch in fetches:
+        fetch.start()
+    for at in range(2):
+
+        @pl.when(sec == at)
+        def _():
+            for m in range(MICRO):
+                load(m, at).start()
+
     r.sm[...] = jnp.zeros_like(r.sm)
-    starts = jnp.where((r.markers[...] > 0) | (iota((MICRO, T), 1) == 0), 1.0, 0.0)
+    for fetch in fetches:
+        fetch.wait()
+    starts = jnp.where((r.v_markers[...] > 0) | (iota((MICRO, T), 1) == 0), 1.0, 0.0)
     starts = jnp.concatenate([starts, jnp.zeros((8 - MICRO, T), f32)], axis=0).T
     for m in range(MICRO):
         r.reset[m] = jnp.broadcast_to(starts[:, m : m + 1], (T, 128))
-    for at in range(2):
-
-        @pl.when(sec == at)
-        def _():
-            for m in range(MICRO):
-                load(m, at).start()
+    def keep(m, at):
+        src, dst = ((r.v_out, r.section_out), (r.v_grad, r.section_grad))[at]
+        return pltpu.make_async_copy(of(src, m), dst.at[m], r.keeps.at[at, m])
 
     def boundary(route, m):
         if route == RIGHT:
-            src, dst, at = r.section_out.at[m], of(r.u, m), 0
+            src, dst, at = of(r.v_out, m), of(r.u, m), 0
         else:
             src, dst, at = of(r.back, m), of(r.go, m), 1
         return remote(src, dst, r.edge.at[at, 0, m], r.edge.at[at, 1, m], dict(section=1 - sec))
 
     if inside:
         tails = r.tails
-        links.greet()
-        part(win, links.i, r1)[...] = r.in_proj[...].astype(bf16)
-        part(wout, links.i, r2)[...] = r.out_proj[0].astype(bf16)
-        head = jnp.concatenate([r.x_proj[...], r.dt_proj[0]], axis=0).T
+        part(win, links.i, r1)[...] = r.v_in_proj[...].astype(bf16)
+        part(wout, links.i, r2)[...] = r.v_out_proj[0].astype(bf16)
+        head = jnp.concatenate([r.v_x_proj[...], r.v_dt_proj[0]], axis=0).T
         part(small, links.i, r2)[...] = head.astype(bf16)
-        top = [r.a_log[...], r.conv_weight[0], r.conv_bias[...], r.dt_bias[...], r.d_skip[...]]
-        top.append(jnp.concatenate([r.norm_gain[...], jnp.zeros((1, r2 - gw), f32)], axis=1))
+        top = [r.v_a_log[...], r.v_conv_weight[0], r.v_conv_bias[...], r.v_dt_bias[...], r.v_d_skip[...]]
+        top.append(jnp.concatenate([r.v_norm_gain[...], jnp.zeros((1, r2 - gw), f32)], axis=1))
         top = jnp.concatenate(top + [jnp.zeros((8, r2), f32)], axis=0)
         top = jnp.concatenate([top, jnp.zeros((32, 128 - r2), f32)], axis=1)
         part(tails, links.i, 32)[...] = top.astype(bf16)
@@ -583,7 +646,7 @@
             (win, r1, half, links.zs),
             (wout, r2, 0, links.zs),
         ]
-        gather = Gather(links, pieces, r.ag_line, r.ag_core, r.ag_recv)
+        gather = Gather(links, pieces, (4,), r.ag_line, r.ag_core, r.ag_recv)
         early, late = (0, 1, 2), (3, 4)
 
         def pass_on(ps, hops):
@@ -594,15 +657,41 @@
                 for p in ps:
                     gather.across(p, hop - 1)
 
-        for p in early + late:
+        for p in early:
             gather.start(p)
-        pass_on(early + late, range(1, links.zs - 1))
-        pass_on(early, range(links.zs - 1, links.zs + 1))
+        for p in late:
+            gather.start(p)
+        for p in early:
+            gather.line(p, 1)
+        for p in late:
+            gather.line(p, 1)
+        for p in early:
+            gather.across(p, 0)
+        for p in early:
+            gather.line(p, 2)
+        for p in late:
+            gather.across(p, 0)
+        for p in early:
+            gather.across(p, 1)
+        for p in early:
+            gather.line(p, 3)
+        for p in late:
+            gather.line(p, 2)
+        for p in early:
+            gather.across(p, 2)
+        for p in late:
+            gather.across(p, 1)
+        for p in early:
+            gather.across(p, 3)
+        for p in late:
+            gather.line(p, 3)
         for p in early:
             gather.arrived(p)
 
         def rest(hops):
-            pass_on(late, hops)
+            for hop in hops:
+                for p in late:
+                    gather.across(p, hop - 1)
             if links.zs in hops:
                 for p in late:
                     gather.arrived(p)
@@ -614,12 +703,12 @@
         weight_rows(tails, rows, gain, n)
         half_rows = 2 * links.zs
         pieces = [
-            (r.gwo, 0, r.co, r.uo, r.do, r.gout_shard, r2, 0, links.zs),
-            (r.gwi, 0, r.ci, r.ui, r.di, r.gin_shard, r1, half, links.zs),
-            (r.gwi, 0, r.ci, r.ui, r.di, r.gin_shard, r1, 0, half),
+            (r.gwo, 0, r.co, r.uo, r.do, r.v_gout, r2, 0, links.zs),
+            (r.gwi, 0, r.ci, r.ui, r.di, r.v_gin, r1, half, links.zs),
+            (r.gwi, 0, r.ci, r.ui, r.di, r.v_gin, r1, 0, half),
             (r.gws, links.x * half_rows * r3, r.cs, None, None, None, r3, 0, links.zs),
         ]
-        scatter = Scatter(links, pieces, r.rs_core, r.rs_line)
+        scatter = Scatter(links, pieces, (1, 2, 2, 1), r.rs_core, r.rs_line)
         strip = 2 * r1
 
         def operand(kind, m, zz=0):
@@ -649,7 +738,7 @@
             sem, inc=1, device_id=dict(section=1 - sec), device_id_type=pl.DeviceIdType.MESH
         )
         pl.semaphore_wait(sem, 1)
-        rows[...] = r.raw_rows[...]
+        rows[...] = r.v_raw_rows[...]
     for c in range(DI // C):
         s = pl.ds(c * C, C)
         rows[0:NS, s] = -jnp.exp(rows[0:NS, s]) * LOG2E
@@ -699,12 +788,13 @@
             )
             f_scan(act, rows, of(r.dec, m), r.gs, r.cols, r.diag, r.h.at[m], ssm)
             gathering((links.zs,))
-            f_out(u, normed, win, wout, ssm, of(r.sz, m), of(r.dz, m), of(r.gated, m), r.section_out.at[m])
+            f_out(u, normed, win, wout, ssm, of(r.sz, m), of(r.dz, m), of(r.gated, m), of(r.v_out, m))
 
             @pl.when(sec == 0)
             def _():
                 boundary(RIGHT, m).start()
 
+            keep(m, 0).start()
             if inside:
                 operand(0, m).start()
                 operand(1, m).start()
@@ -728,10 +818,13 @@
             for kind in (0, 2):
                 for m in range(MICRO):
                     operand(kind, m).wait_recv()
+            def mine(ref, zz):
+                at = zz * 4 * r2
+                return jnp.where(links.x == 0, ref[:, at : at + 2 * r2], ref[:, at + 2 * r2 : at + 4 * r2])
+
             for zz in range(links.zs):
-                s = pl.ds(zz * 4 * r2, 4 * r2)
-                full = tn(r.gated[:, s], r.go[...]) + tn(r.xg[:, s], r.xo[...])
-                owners_rows(r.gwo, 0, r2, zz, jnp.where(links.x == 0, full[: 2 * r2], full[2 * r2 :]))
+                value = tn(mine(r.gated, zz), r.go[...]) + tn(mine(r.xg, zz), r.xo[...])
+                owners_rows(r.gwo, 0, r2, zz, value)
         else:
             for c in range(DI // C):
                 s = pl.ds(c * C, C)
@@ -838,7 +931,7 @@
                 for zz in low:
                     operand(3, m, zz).start()
                 early(products_head)
-            sg = r.section_grad.at[m]
+            sg = of(r.v_grad, m)
             b_in(first, of(r.u, m), go, gain, win, gm, sg, r.gg)
 
             @pl.when(sec == 1)
@@ -846,6 +939,7 @@
                 of(r.back, m)[...] = sg[...].astype(bf16)
                 boundary(LEFT, m).start()
 
+            keep(m, 1).start()
             if inside:
                 early(fourth_step)
 
@@ -888,17 +982,6 @@
         def _():
             scatter.line(2)
 
-        small_direct(lambda copy: copy.wait_recv())
-        total_small = scatter.mine(3, links.z)[...].astype(f32)
-        for step in range(1, links.zs):
-            total_small = total_small + part(r.ss, step, r3)[...].astype(f32)
-        r.gsmall_shard[...] = total_small
-        for p in range(3):
-            scatter.own(p)
-        for p in range(3):
-            scatter.finish(p)
-        scatter.copy(3, CORE).wait_send()
-        small_direct(lambda copy: copy.wait_send())
         for p in range(len(gather.pieces)):
             gather.finish(p)
         for m in range(MICRO):
@@ -907,10 +990,38 @@
             for zz in range(links.zs):
                 operand(3, m, zz).wait_send()
         small_across().wait_send()
+        results = [
+            pltpu.make_async_copy(src, dst, r.fetch.at[at])
+            for at, (src, dst) in enumerate(
+                ((r.v_gsmall, r.gsmall_shard), (r.v_gout, r.gout_shard), (r.v_gin, r.gin_shard))
+            )
+        ]
+        small_direct(lambda copy: copy.wait_recv())
+        total_small = scatter.mine(3, links.z)[...].astype(f32)
+        for step in range(1, links.zs):
+            total_small = total_small + part(r.ss, step, r3)[...].astype(f32)
+        r.v_gsmall[...] = total_small
+        results[0].start()
+        scatter.own(0)
+        results[1].start()
+        scatter.finish(0)
+        small_direct(lambda copy: copy.wait_send())
+        scatter.copy(3, CORE).wait_send()
+        scatter.own(1)
+        scatter.finish(1)
+        scatter.own(2)
+        results[2].start()
+        scatter.finish(2)
+        for result in results:
+            result.wait()
     else:
         products_out()
         products_in(None)
         products_head()
+
+    for m in range(MICRO):
+        for at in range(2):
+            keep(m, at).wait()
 
     for m in range(MICRO):
 
@@ -960,8 +1071,10 @@
         cols=((T * NS, 128), f32),
         diag=((T, NS * TB), bf16),
         rows=((32, DI), f32),
+        gain=((1, D), f32),
     )
-    sems = dict(edge=(2, 2, MICRO), loads=(MICRO,))
+    scratch |= dict(v_out=((rows2, D), bf16), v_grad=((rows2, D), f32), v_markers=((MICRO, T), jnp.int32))
+    sems = dict(edge=(2, 2, MICRO), loads=(MICRO,), keeps=(2, MICRO), fetch=(12,))
     if inside:
         outs |= dict(
             gin_shard=((r1, D), f32),
@@ -969,8 +1082,20 @@
             gsmall_shard=((r2 + 32, 128), f32),
         )
         scratch |= dict(
+            v_norm_gain=((1, D // n), f32),
+            v_in_proj=((r1, D), f32),
+            v_conv_weight=((1, KC, r2), f32),
+            v_conv_bias=((1, r2), f32),
+            v_x_proj=((RK + 2 * NS, r2), f32),
+            v_dt_proj=((1, RK, r2), f32),
+            v_dt_bias=((1, r2), f32),
+            v_a_log=((NS, r2), f32),
+            v_d_skip=((1, r2), f32),
+            v_out_proj=((1, r2, D), f32),
+            v_gin=((r1, D), f32),
+            v_gout=((r2, D), f32),
+            v_gsmall=((r2 + 32, 128), f32),
             sm=((32, DI), f32),
-            gain=((1, D), f32),
             gg=((1, D), f32),
             win=((2 * DI, D), bf16),
             wout=((DI, D), bf16),
@@ -995,11 +1120,11 @@
             do=((zs * r2, D), bf16),
         )
         sems |= dict(
-            ag_line=(5, 3, zs),
+            ag_line=(5, 4, zs),
             ag_core=(5, 2 * zs),
             ag_recv=(5, n),
             rs_core=(4, 2),
-            rs_line=(3, 4, zs),
+            rs_line=(3, 8, zs),
             xs_sems=(8, max(MICRO, zs), 2),
         )
     else:
@@ -1010,14 +1135,20 @@
             gg=((1, D), f32),
             sm=((32, DI), f32),
         )
+        scratch |= dict(
+            win=((2 * DI, D), bf16),
+            wout=((DI, D), bf16),
+            small=((DI, 128), bf16),
+            v_raw_rows=((32, DI), f32),
+        )
     names = list(arrays) + list(outs) + list(scratch) + list(sems)
     whole = pl.BlockSpec(memory_space=pltpu.VMEM)
     far = pl.BlockSpec(memory_space=pl.ANY)
     results = pl.pallas_call(
         functools.partial(block, names, inside, n),
         out_shape=[jax.ShapeDtypeStruct(*spec) for spec in outs.values()],
-        in_specs=[far] * 2 + [whole] * (len(arrays) - 2),
-        out_specs=[whole] * len(outs),
+        in_specs=[far] * len(arrays),
+        out_specs=[far] * len(outs) if inside else [far] * 2 + [whole] * (len(outs) - 2),
         scratch_shapes=[pltpu.VMEM(*spec) for spec in scratch.values()]
         + [pltpu.SemaphoreType.DMA(shape) for shape in sems.values()],
         compiler_params=pltpu.CompilerParams(
@@ -1106,11 +1237,11 @@
         [a_log[0].T, conv_weight[0], conv_bias, dt_bias, d_skip, jnp.zeros((9, r2), f32)], axis=0
     )
     arrays |= dict(
-        win=gathered(in_proj[0].T, 0),
-        wout=gathered(out_proj[0], 0),
-        small=gathered(jnp.concatenate([x_proj[0], dt_proj[0].T], axis=1), 0),
+        all_win=gathered(in_proj[0].T, 0),
+        all_wout=gathered(out_proj[0], 0),
+        all_small=gathered(jnp.concatenate([x_proj[0], dt_proj[0].T], axis=1), 0),
         raw_rows=gathered(raw, 1).astype(f32),
-        gain=gathered(norm_gain, 1).astype(f32),
+        all_gain=gathered(norm_gain, 1).astype(f32),
     )
     res = call(n, inside, arrays)
 

time: 177 us -> 169 us (0.955)
  Pallas kernels: 176 us -> 168 us
    pallas_call x1, Pallas kernels: 174 us -> 165 us  [call(): pl.pallas_call(functools.partial(block, names, inside, n), out_shape=[jax...]
where the time goes in v4:
time: 169 us
  Pallas kernels  168 us (99%)
    pallas_call x1, Pallas kernels, call(): pl.pallas_call(functools.partial(block, names, inside, n), out_shape=[jax...  165 us

profile of v4, /device:TPU:0, one launch (start us, length us, event | category | flops | bytes accessed | tf_op | source)
XLA Modules:
  0.0 168.7 jit_solution(13109409939668421483)
XLA Ops:
  0.6 165.1 %two_layer_block.1 = (bf16[2,128,768]{2,1,0:T(8,128)(2,1)}, f32[2,128,768]{2,1,0:T(8,128)}, f32[192,768]{1,0:T(8,128)}, f32[96,768]{1,0:T(8,128)}, f32[128,128]{1,0:T(8,128)}) custom-call(bf16[2,128,768]{2,1,0:T(8,128)(2,1)} %refs_0_.1, bf16[2,128,768]{2,1,0:T(8,128)(2,1)} %refs_1_.1, s32[2,128]{1,0:T(2,128)} %refs_2_.1, f32[1,48]{1,0:T(1,128)} %refs_3_.1, ...), custom_call_target="tpu_custom_call" | custom-call | tf_op jit(solution)/shard_map/two_layer_block/pallas_call | solution.py:1147
  165.7 2.9 %unpack.1 = (bf16[1,2,128,768]{3,2,1,0:T(8,128)(2,1)}, f32[1,2,128,768]{3,2,1,0:T(8,128)}, f32[1,48]{1,0:T(1,128)}, f32[192,768]{1,0:T(8,128)}, f32[1,4,96]{2,1,...) custom-call(bf16[2,128,768]{2,1,0:T(8,128)(2,1)} %get-tuple-element., ...), custom_call_target="tpu_custom_call" | custom-call | tf_op jit(solution)/shard_map/unpack/pallas_call | solution.py:1216

commit v5 on v4

--- a/solution.py
+++ b/solution.py
@@ -49,7 +49,7 @@
 
 
 def sigmoid(v):
-    return 1.0 / (1.0 + jnp.exp(-v))
+    return 0.5 * jnp.tanh(0.5 * v) + 0.5
 
 
 def wide(v):
@@ -129,14 +129,14 @@
         lax.fori_loop(0, NB, block, jnp.zeros((NS, CS), f32))
 
     def sums(i, carry):
-        for q in range(4):
-            t0 = pl.multiple_of(i * (4 * TB) + q * TB, TB)
+        for q in range(8):
+            t0 = pl.multiple_of(i * (8 * TB) + q * TB, TB)
             tt = pl.ds(t0, TB)
             y = nn(diag[tt, :], h_ref[pl.ds(t0 * NS + NS, TB * NS), :])
             ssm[tt, :] = y + rows[22:23, :] * act[tt, :].astype(f32)
         return carry
 
-    lax.fori_loop(0, NB // 4, sums, 0)
+    lax.fori_loop(0, NB // 8, sums, 0)
 
 
 def f_out(u, normed, win, wout, ssm, sz_ref, dz_ref, gated, out):
@@ -176,19 +176,19 @@
     diag[...] = block_diagonal(p[:, RK : RK + NS])
 
 
-def b_scan(between, first, gs, rows, dec, cols, diag, drive, h_ref, adj_ref, gd, gr, gb, gc, sm):
+def b_scan(between, first, gs, rows, dec, cols, diag, drive, h_ref, adj_ref, ea_ref, gd, gr, gb, gc, sm):
     ones = (iota((TB, TB * NS), 1) // NS) == iota((TB, TB * NS), 0)
-    od = ones.astype(bf16)
+    od = (iota((TB, TB * NS // 2), 1) // (NS // 2) == iota((TB, TB * NS // 2), 0)).astype(bf16)
 
     def state_sums(i, carry):
-        for q in range(4):
-            t0 = pl.multiple_of(i * (4 * TB) + q * TB, TB)
+        for q in range(8):
+            t0 = pl.multiple_of(i * (8 * TB) + q * TB, TB)
             tt = pl.ds(t0, TB)
             full = nt(gs[tt, :].astype(bf16), h_ref[pl.ds(t0 * NS + NS, TB * NS), :])
             gc[tt, :] = jnp.where(ones, full, 0.0).astype(bf16)
         return carry
 
-    lax.fori_loop(0, NB // 4, state_sums, 0)
+    lax.fori_loop(0, NB // 8, state_sums, 0)
     for c in range(DI // CS):
         s = pl.ds(c * CS, CS)
 
@@ -198,6 +198,7 @@
             a2 = rows[0:NS, s]
             d = dec[pl.ds(t0, TB), s]
             g = gs[pl.ds(t0, TB), s]
+            later = None
             for j in reversed(range(TB)):
                 row = pl.ds(t0 * NS + j * NS, NS)
                 adj = g[j : j + 1, :] * wide(cols[row, :]) + carry
@@ -205,7 +206,13 @@
                 dj = d[j : j + 1, :]
                 carry = jnp.exp2(dj * a2) * adj
                 expo = carry * h_ref[row, s].astype(f32)
-                h_ref[row, s] = (expo * a2).astype(bf16)
+                weighted = expo * a2
+                weighted = weighted[0 : NS // 2] + weighted[NS // 2 :]
+                if j % 2:
+                    later = weighted
+                else:
+                    pair = pl.ds(pl.multiple_of(t0 * (NS // 2), NS) + j * (NS // 2), NS)
+                    ea_ref[pair, :] = jnp.concatenate([weighted, later], axis=0).astype(bf16)
                 acc = acc + expo * dj
             return carry, acc
 
@@ -214,17 +221,25 @@
         sm[0:NS, s] = total(sm[0:NS, s], first, acc * rows[0:NS, s] * LN2)
 
         def adjoint_sums(i, carry):
-            for q in range(4):
-                t0 = pl.multiple_of(i * (4 * TB) + q * TB, TB)
+            for q in range(8):
+                t0 = pl.multiple_of(i * (8 * TB) + q * TB, TB)
                 tt = pl.ds(t0, TB)
                 row = pl.ds(t0 * NS, TB * NS)
                 gd[tt, s] = nn(diag[tt, :], adj_ref[row, :])
-                gr[tt, s] = nn(od, h_ref[row, s]) * LN2
+            for q in range(8):
+                t0 = pl.multiple_of(i * (8 * TB) + q * TB, TB)
+                tt = pl.ds(t0, TB)
+                ea = ea_ref[pl.ds(pl.multiple_of(t0 * (NS // 2), NS), TB * NS // 2), :]
+                gr[tt, s] = nn(od, ea) * LN2
+            for q in range(8):
+                t0 = pl.multiple_of(i * (8 * TB) + q * TB, TB)
+                tt = pl.ds(t0, TB)
+                row = pl.ds(t0 * NS, TB * NS)
                 full = nt(drive[tt, s], adj_ref[row, :])
                 gb[tt, :] = full if c == 0 else gb[tt, :] + full
             return carry
 
-        lax.fori_loop(0, NB // 4, adjoint_sums, 0)
+        lax.fori_loop(0, NB // 8, adjoint_sums, 0)
         if c == 0 and between is not None:
             between()
 
@@ -921,7 +936,7 @@
             b_prep(of(r.proj, m), r.cols, r.diag)
             b_scan(
                 (lambda: early(first_products)) if inside else None,
-                first, gs, rows, dec, r.cols, r.diag, of(r.drive, m), r.h.at[m], r.adj, gd, gr, gb, gc, sm
+                first, gs, rows, dec, r.cols, r.diag, of(r.drive, m), r.h.at[m], r.adj, r.ea, gd, gr, gb, gc, sm
             )
             if inside:
                 early(second_products)
@@ -1062,6 +1077,7 @@
         gp=((rows2, 128), bf16),
         h=((MICRO, (T + 1) * NS, DI), bf16),
         adj=((T * NS, CS), bf16),
+        ea=((T * NS // 2, CS), bf16),
         dec=((rows2, DI), f32),
         gs=((T, DI), f32),
         gr=((T, DI), f32),
@@ -1159,24 +1175,40 @@
     return types.SimpleNamespace(**dict(zip(outs, results)))
 
 
-def unpack(
-    out, grad, gin, gout, gsmall, out_o, grad_o, gain_o, in_o, cw_o, cb_o, x_o, dt_o, db_o, a_o, ds_o, po_o
-):
+def unpack(*refs):
+    far_in, far_out, near_in, near_out, sems = refs[:5], refs[5:17], refs[17:22], refs[22:31], refs[31]
+    gsmall = near_in[4]
+    gain_o, in_o, cw_o, cb_o, x_o, dt_o, db_o, a_o, ds_o = near_out
+    loads = [pltpu.make_async_copy(far, near, sems.at[0, at]) for at, (far, near) in enumerate(zip(far_in, near_in))]
+    for at in (4, 1, 0, 2, 3):
+        loads[at].start()
+    stores = []
+
+    def store(src, at):
+        stores.append(pltpu.make_async_copy(src, far_out[at], sems.at[1, at]))
+        stores[-1].start()
+
+    loads[4].wait()
     r2, gw = cb_o.shape[1], gain_o.shape[1]
-    out_o[0] = out[...]
-    grad_o[0] = grad[...]
-    po_o[0] = gout[...]
-    in_o[...] = gin[...]
     tail = gsmall[pl.ds(r2, 32), :]
+    small = gsmall[pl.ds(0, r2), :].T
     gain_o[...] = tail[23:24, 0:gw]
     cw_o[0] = tail[NS : NS + KC, 0:r2]
     cb_o[...] = tail[20:21, 0:r2]
     db_o[...] = tail[21:22, 0:r2]
     ds_o[...] = tail[22:23, 0:r2]
     a_o[...] = tail[0:NS, 0:r2]
-    small = gsmall[pl.ds(0, r2), :].T
     x_o[...] = small[0 : RK + 2 * NS, :]
     dt_o[0] = small[RK + 2 * NS : 128, :]
+    for src, at in ((gain_o, 2), (cw_o, 4), (cb_o, 5), (x_o, 6), (dt_o, 7), (db_o, 8), (a_o, 9), (ds_o, 10)):
+        store(src, at)
+    for src, at in ((1, 1), (0, 0), (2, 3), (3, 11)):
+        loads[src].wait()
+        far = far_out[at] if at == 3 else far_out[at].at[0]
+        stores.append(pltpu.make_async_copy(near_in[src], far, sems.at[1, at]))
+        stores[-1].start()
+    for copy in stores:
+        copy.wait()
 
 
 def on_device(inputs, cotangent, markers, *weights):
@@ -1209,23 +1241,21 @@
             out_proj=out_proj,
         )
         res = call(n, inside, arrays)
-        whole = pl.BlockSpec(memory_space=pltpu.VMEM)
+        far = pl.BlockSpec(memory_space=pl.ANY)
         turned = (in_proj, x_proj, a_log)
         shapes = [((1,) + res.section_out.shape, bf16), ((1,) + res.section_grad.shape, f32)]
         shapes += [(w.shape[:0:-1] if any(w is t for t in turned) else w.shape, f32) for w in weights]
+        parts = (res.section_out, res.section_grad, res.gin_shard, res.gout_shard, res.gsmall_shard)
         done = pl.pallas_call(
             unpack,
             out_shape=[jax.ShapeDtypeStruct(*spec) for spec in shapes],
-            in_specs=[whole] * 5,
-            out_specs=[whole] * 12,
+            in_specs=[far] * 5,
+            out_specs=[far] * 12,
+            scratch_shapes=[pltpu.VMEM(part.shape, part.dtype) for part in parts]
+            + [pltpu.VMEM(*spec) for spec in shapes[2:11]]
+            + [pltpu.SemaphoreType.DMA((2, 12))],
             name="unpack",
-        )(
-            res.section_out,
-            res.section_grad,
-            res.gin_shard,
-            res.gout_shard,
-            res.gsmall_shard,
-        )
+        )(*parts)
         grads = (g.T[None] if any(w is t for t in turned) else g for w, g in zip(weights, done[2:]))
         return (*done[:2], *grads)
 

time: 169 us -> 165 us (0.976)
  Pallas kernels: 168 us -> 164 us
    pallas_call x1, Pallas kernels: 165 us -> 161 us  [call(): pl.pallas_call(functools.partial(block, names, inside, n), out_shape=[jax...]
where the time goes in v5:
time: 165 us
  Pallas kernels  164 us (99%)
    pallas_call x1, Pallas kernels, call(): pl.pallas_call(functools.partial(block, names, inside, n), out_shape=[jax...  161 us

profile of v5, /device:TPU:0, one launch (start us, length us, event | category | flops | bytes accessed | tf_op | source)
XLA Modules:
  0.0 165.0 jit_solution(10386787868938551453)
XLA Ops:
  0.6 161.4 %two_layer_block.1 = (bf16[2,128,768]{2,1,0:T(8,128)(2,1)}, f32[2,128,768]{2,1,0:T(8,128)}, f32[192,768]{1,0:T(8,128)}, f32[96,768]{1,0:T(8,128)}, f32[128,128]{1,0:T(8,128)}) custom-call(bf16[2,128,768]{2,1,0:T(8,128)(2,1)} %refs_0_.1, bf16[2,128,768]{2,1,0:T(8,128)(2,1)} %refs_1_.1, s32[2,128]{1,0:T(2,128)} %refs_2_.1, f32[1,48]{1,0:T(1,128)} %refs_3_.1, ...), custom_call_target="tpu_custom_call" | custom-call | tf_op jit(solution)/shard_map/two_layer_block/pallas_call | solution.py:1163
  162.1 2.7 %unpack.1 = (bf16[1,2,128,768]{3,2,1,0:T(8,128)(2,1)}, f32[1,2,128,768]{3,2,1,0:T(8,128)}, f32[1,48]{1,0:T(1,128)}, f32[192,768]{1,0:T(8,128)}, f32[1,4,96]{2,1,...) custom-call(bf16[2,128,768]{2,1,0:T(8,128)(2,1)} %get-tuple-element., ...), custom_call_target="tpu_custom_call" | custom-call | tf_op jit(solution)/shard_map/unpack/pallas_call | solution.py:1249

commit v6 on v5

--- a/solution.py
+++ b/solution.py
@@ -912,6 +912,8 @@
 
         @pl.when((m >= 0) & (m < MICRO))
         def _():
+            b_prep(of(r.proj, m), r.cols, r.diag)
+
             @pl.when(sec == 0)
             def _():
                 boundary(LEFT, m).wait_recv()
@@ -933,7 +935,6 @@
             if inside:
                 for zz in high:
                     operand(3, m, zz).start()
-            b_prep(of(r.proj, m), r.cols, r.diag)
             b_scan(
                 (lambda: early(first_products)) if inside else None,
                 first, gs, rows, dec, r.cols, r.diag, of(r.drive, m), r.h.at[m], r.adj, r.ea, gd, gr, gb, gc, sm

time: 165 us -> 166 us (level)
  no operation moved by 1% of the time
where the time goes in v6:
time: 166 us; the launch traced here: 165 us
  Pallas kernels  165 us (99%)
    pallas_call x1, Pallas kernels, call(): pl.pallas_call(functools.partial(block, names, inside, n), out_shape=[jax...  162 us

profile of v6, /device:TPU:0, one launch (start us, length us, event | category | flops | bytes accessed | tf_op | source)
XLA Modules:
  0.0 165.4 jit_solution(4047251538394871660)
XLA Ops:
  0.6 161.9 %two_layer_block.1 = (bf16[2,128,768]{2,1,0:T(8,128)(2,1)}, f32[2,128,768]{2,1,0:T(8,128)}, f32[192,768]{1,0:T(8,128)}, f32[96,768]{1,0:T(8,128)}, f32[128,128]{1,0:T(8,128)}) custom-call(bf16[2,128,768]{2,1,0:T(8,128)(2,1)} %refs_0_.1, bf16[2,128,768]{2,1,0:T(8,128)(2,1)} %refs_1_.1, s32[2,128]{1,0:T(2,128)} %refs_2_.1, f32[1,48]{1,0:T(1,128)} %refs_3_.1, ...), custom_call_target="tpu_custom_call" | custom-call | tf_op jit(solution)/shard_map/two_layer_block/pallas_call | solution.py:1164
  162.5 2.7 %unpack.1 = (bf16[1,2,128,768]{3,2,1,0:T(8,128)(2,1)}, f32[1,2,128,768]{3,2,1,0:T(8,128)}, f32[1,48]{1,0:T(1,128)}, f32[192,768]{1,0:T(8,128)}, f32[1,4,96]{2,1,...) custom-call(bf16[2,128,768]{2,1,0:T(8,128)(2,1)} %get-tuple-element., ...), custom_call_target="tpu_custom_call" | custom-call | tf_op jit(solution)/shard_map/unpack/pallas_call | solution.py:1250
